TPU v7x, 128 devices: a whole 4x4x4 slice. The times are simulated.
128 devices in a mesh: replica: 4 (over x), section: 2 (over y_lo), tensor: 16 (over z, y_hi, core).
Axes of the slice: x: 4, y: 4 (y_hi: 2, y_lo: 2; y = y_hi * 2 + y_lo), z: 4, core: 2. Of those that a mesh axis runs over, the one named last changes fastest.
Arguments:
- boundary: bfloat16 [4, 2, 128, 4, 8192], P('replica', 'section', 'tensor'), may hold values from -6 to 6
- context: bfloat16 [4, 2, 128, 4, 4096], P('replica', 'section', None, None, 'tensor'), may hold values from -6 to 6
- weights: bfloat16 [4, 2, 4096, 8192], P('replica', 'section', 'tensor'), may hold values from -0.09375 to 0.09375
- momentum: bfloat16 [4, 2, 4096, 8192], P('replica', 'section', 'tensor'), may hold values from -0.119628906 to 0.119628906
- route: int32 [4, 2], replicated, may hold values from 0 to 3, as said below
- partner: int32 [4, 2], replicated, may hold values from 0 to 3, as said below
Outputs:
- stream_out: bfloat16 [4, 2, 128, 4, 8192], P('replica', 'section', 'tensor')
- context_grad: bfloat16 [4, 2, 128, 4, 4096], P('replica', 'section', None, None, 'tensor')
- new_weights: bfloat16 [4, 2, 4096, 8192], P('replica', 'section', 'tensor')
- new_momentum: bfloat16 [4, 2, 4096, 8192], P('replica', 'section', 'tensor')
Inputs may be any that keep to these rules, and one draw needn't show every extreme that they name: `route`: every replica's section 1 takes at most 4 micro-batches, and in every draw one replica takes exactly 4. For each section s, partner[., s] is a permutation of the replicas with partner[r, s] != r, and the offsets (partner[r, s] - r) mod 4 take every value from 1 to 3.
All inputs are finite; a program needn't handle non-finite values.
Results may differ from a plain program's by a relative error of at most 0.017.
Values may be sent and summed in bfloat16 or wider, within the bound.
A program may use at most 192 MiB of HBM per device.

v0:
```python
import math

import jax
import jax.numpy as jnp
from jax import lax
from jax.sharding import PartitionSpec as P

ALPHA = 0.9
GAMMA = 0.5
BETA_SCALE = 0.4


def passed_along(array, axis, by):
    devices = lax.axis_size(axis)
    pairs = [(i, i + by) for i in range(devices) if 0 <= i + by < devices]
    return lax.ppermute(array, axis, pairs)


def local(boundary, context, weights, momentum, route, partner):
    section_here = lax.axis_index("section")
    replica_here = lax.axis_index("replica")
    replicas = lax.axis_size("replica")
    boundary = boundary[0, 0]
    context = context[0, 0]
    weights = weights[0, 0]
    momentum = momentum[0, 0]
    row_count, capacity, model_width = boundary.shape
    token_count = context.shape[0]
    micro_count = route.shape[1]
    owners = jnp.arange(replicas, dtype=jnp.int32)
    arrivals = (route.reshape(-1)[None, :] == owners[:, None]).astype(jnp.int32)
    slot_index = jnp.cumsum(arrivals, axis=1) - 1
    own_arrivals = lax.dynamic_index_in_dim(arrivals, replica_here, 0, keepdims=False)
    own_slots = lax.dynamic_index_in_dim(slot_index, replica_here, 0, keepdims=False)
    places = jnp.arange(capacity, dtype=jnp.int32)
    select = ((own_arrivals[None, :] == 1) & (own_slots[None, :] == places[:, None])).astype(
        jnp.bfloat16
    )
    select = select.reshape(capacity, replicas, micro_count)
    live_count = jnp.where(section_here == 0, micro_count, jnp.sum(own_arrivals))
    live_slots = (places < live_count)[None, :, None]
    own_route = lax.dynamic_index_in_dim(route, replica_here, 0, keepdims=False)
    dest_mask = (own_route[None, :] == owners[:, None]).astype(jnp.bfloat16)
    zero_rows = jnp.zeros_like(boundary)
    cot_own = jnp.where(live_slots, boundary, zero_rows)
    back_buffer = jnp.einsum(
        "krm,tkd->rtmd", select, cot_own, preferred_element_type=jnp.float32
    ).astype(jnp.bfloat16)
    moved_back = passed_along(back_buffer, "section", -1)
    returned = lax.all_to_all(moved_back, "replica", split_axis=0, concat_axis=0, tiled=True)
    first_cot = jnp.sum(returned, axis=0, dtype=jnp.float32).astype(jnp.bfloat16)
    padding = jnp.zeros((row_count, capacity - micro_count, model_width), jnp.bfloat16)
    first_cot = jnp.concatenate([first_cot, padding], axis=1)
    cot_here = jnp.where(section_here == 0, first_cot, cot_own)
    ctx_rows = context
    branch_sum = lax.psum_scatter(
        jnp.einsum("tkh,hd->tkd", ctx_rows, weights, preferred_element_type=jnp.float32).astype(
            jnp.bfloat16
        ),
        "tensor",
        scatter_dimension=0,
        tiled=True,
    ).astype(jnp.float32)
    own_stream = (boundary.astype(jnp.float32) + branch_sum).astype(jnp.bfloat16)
    forward_buffer = dest_mask[:, None, :, None] * own_stream[None, :, :micro_count, :]
    moved_ahead = passed_along(forward_buffer, "section", 1)
    arrived = lax.all_to_all(moved_ahead, "replica", split_axis=0, concat_axis=0, tiled=True)
    incoming = jnp.einsum("krm,rtmd->tkd", select, arrived, preferred_element_type=jnp.float32)
    routed_stream = (incoming + branch_sum).astype(jnp.bfloat16)
    stream_out = jnp.where(section_here == 0, own_stream, routed_stream)
    stream_out = jnp.where(live_slots, stream_out, zero_rows)
    row_piece = lax.all_gather(cot_here, "tensor", axis=0, tiled=True)
    ctx_rows = context
    grad_sum = jnp.einsum("tkh,tkd->hd", ctx_rows, row_piece, preferred_element_type=jnp.float32)
    ctx_block = jnp.einsum(
        "tkd,hd->tkh", row_piece, weights, preferred_element_type=jnp.float32
    ).astype(jnp.bfloat16)
    ctx_grad = ctx_block
    grad_sum, ctx_grad = (grad_sum, ctx_grad)
    current = weights.astype(jnp.float32)
    grad_scale = BETA_SCALE / math.sqrt(token_count * capacity)
    message = (grad_scale * grad_sum - GAMMA * current).astype(jnp.bfloat16)
    partner_row = lax.dynamic_index_in_dim(partner, replica_here, 0, keepdims=False)
    partner_index = lax.dynamic_index_in_dim(partner_row, section_here, 0, keepdims=False)
    gathered = lax.all_gather(message[None], "replica", axis=0, tiled=True)
    partner_message = lax.dynamic_index_in_dim(gathered, partner_index, 0, keepdims=False)
    step_delta = (
        ALPHA * momentum.astype(jnp.float32)
        - 0.5 * (grad_scale * grad_sum + GAMMA * current)
        - 0.5 * partner_message.astype(jnp.float32)
    )
    new_momentum = step_delta.astype(jnp.bfloat16)
    new_weights = (current + step_delta).astype(jnp.bfloat16)
    return (
        stream_out[None, None],
        ctx_grad[None, None],
        new_weights[None, None],
        new_momentum[None, None],
    )


def solution(mesh):
    in_specs = (
        P("replica", "section", "tensor", None, None),
        P("replica", "section", None, None, "tensor"),
        P("replica", "section", "tensor", None),
        P("replica", "section", "tensor", None),
        P(),
        P(),
    )
    out_specs = (
        P("replica", "section", "tensor", None, None),
        P("replica", "section", None, None, "tensor"),
        P("replica", "section", "tensor", None),
        P("replica", "section", "tensor", None),
    )
    return jax.shard_map(local, mesh=mesh, in_specs=in_specs, out_specs=out_specs, check_vma=False)
```

profile of v0, /device:TPU:8, one launch (start us, length us, event | category | flops | bytes accessed | tf_op | source)
XLA Modules:
  0.0 478.5 jit_solution(13371283950068853053)
XLA Ops:
  10.0 1.9 fusion.5
  11.9 2.3 collective-permute-start.1
  14.3 21.6 %collective-permute-done.1 = bf16[4,8,2,8192]{3,0,2,1:T(4,128)(2,1)S(1)} collective-permute-done((bf16[4,8,2,8192]{3,0,2,1:T(4,128)(2,1)S(1)}, bf16[4,8,2,8192]{3,0,2,1:T(4,128)(2,1)S(1)}, u32[]{:S(2)}, u32[]{:S(2)}) %collective-permute-start.1) | collective-permute-done | bytes 1048608 | tf_op jit(solution)/shard_map/ppermute | solution.py:16
  37.0 19.1 %all_to_all.10 = bf16[4,8,2,8192]{3,2,1,0:T(2,128)(2,1)S(1)} all-to-all(bf16[4,8,2,8192]{3,2,1,0:T(2,128)(2,1)S(1)} %copy.80), channel_id=1, replica_groups=mesh['replica'=4,'section'=2,'tensor'=16] {'replica'}, dimensions={0} | all-to-all | bytes 2097152 | tf_op jit(solution)/shard_map/all_to_all | solution.py:50
  57.6 2.3 fusion.34
  60.0 7.8 %fusion = bf16[4,16,8,8192]{3,2,1,0:T(8,128)(2,1)} fusion(bf16[1,1,256,8192]{3,2,1,0:T(8,128)(2,1)} %param.8, bf16[128,4,256]{2,1,0:T(4,128)(2,1)S(1)} %bitcast.102), kind=kOutput, calls=%fused_computation.1 | convolution fusion | flops 2151677952 | bytes 12845056 | tf_op jit(solution)/shard_map/tkh,hd->tkd/dot_general | solution.py:57
  67.7 7.6 %copy.103 = bf16[4,16,8,8192]{3,2,0,1:T(8,128)(2,1)} copy(bf16[4,16,8,8192]{3,2,1,0:T(8,128)(2,1)} %fusion) | data formatting | bytes 16777216
  75.5 6.4 %copy.73 = bf16[1,1,256,8192]{2,3,1,0:T(8,128)(2,1)} copy(bf16[1,1,256,8192]{3,2,1,0:T(8,128)(2,1)} %param.8) | data formatting | bytes 8388608 | tf_op args[2]
  81.9 52.9 %all-gather.4.cloned.1.call-done = bf16[128,4,8192]{2,1,0:T(4,128)(2,1)} async-done(((bf16[8,4,8192]{2,1,0:T(4,128)(2,1)}), bf16[128,4,8192]{2,1,0:T(4,128)(2,1)}) %all-gather.4.cloned.1.call-update) | async-done | bytes 8388624 | tf_op jit(solution)/shard_map/all_gather | solution.py:72
  134.8 18.7 %fusion.14 = (bf16[256,8192]{0,1:T(8,128)(2,1)}, f32[256,8192]{0,1:T(8,128)}) fusion(bf16[1,1,256,8192]{2,3,1,0:T(8,128)(2,1)} %copy.73, bf16[128,4,256]{2,1,0:T(4,128)(2,1)S(1)} %bitcast.103, bf16[128,4,8192]{2,1,0:T(4,128)(2,1)} %all-gather.4.cloned.1.call-done), kind=kOutput, calls=%fused_computation.20 | convolution fusion | flops 2157969408 | bytes 25427968 | tf_op jit(solution)/shard_map/tkh,tkd->hd/dot_general | solution.py:74
  153.8 85.4 %reduce-scatter.4.cloned.1.call-done = bf16[8,32768]{1,0:T(8,128)(2,1)} async-done(((bf16[128,32768]{1,0:T(8,128)(2,1)}), bf16[8,32768]{1,0:T(8,128)(2,1)}) %reduce-scatter.4.cloned.1.call-update) | async-done | bytes 524304
  239.2 1.6 fusion.32
  243.2 24.6 %collective-permute-done = bf16[4,8,2,8192]{3,2,1,0:T(2,128)(2,1)} collective-permute-done((bf16[4,8,2,8192]{3,2,1,0:T(2,128)(2,1)S(1)}, bf16[4,8,2,8192]{3,2,1,0:T(2,128)(2,1)}, u32[]{:S(2)}, u32[]{:S(2)}) %collective-permute-start) | collective-permute-done | bytes 1048608 | tf_op jit(solution)/shard_map/ppermute | solution.py:16
  267.8 4.3 all-to-all-start
  274.0 6.4 %copy.84 = bf16[1,1,256,8192]{2,3,1,0:T(8,128)(2,1)} copy(bf16[1,1,256,8192]{3,2,1,0:T(8,128)(2,1)} %param.9) | data formatting | bytes 8388608 | tf_op args[3]
  281.1 17.7 %all-to-all-done = bf16[4,8,2,8192]{3,2,1,0:T(2,128)(2,1)S(1)} async-done(((bf16[4,8,2,8192]{3,2,1,0:T(2,128)(2,1)}), bf16[4,8,2,8192]{3,2,1,0:T(2,128)(2,1)S(1)}, u32[]{:S(2)}, u32[]{:S(2)}) %all-to-all-start) | async-done | bytes 1048608 | tf_op jit(solution)/shard_map/all_to_all | solution.py:67
  298.7 2.8 fusion.10
  301.5 13.9 %fusion.27 = bf16[1,1,128,4,256]{4,2,3,1,0:T(8,128)(2,1)S(1)} fusion(bf16[1,1,256,8192]{3,2,1,0:T(8,128)(2,1)} %param.8, bf16[128,4,8192]{2,1,0:T(4,128)(2,1)} %all-gather.4.cloned.1.call-done), kind=kOutput, calls=%fused_computation.31 | convolution fusion | flops 2147614720 | bytes 12845056 | tf_op jit(solution)/shard_map/tkd,hd->tkh/dot_general | solution.py:75
  316.4 94.2 %all-gather.6.cloned.1.call-done = bf16[1024,8192]{0,1:T(8,128)(2,1)} async-done(((bf16[256,8192]{0,1:T(8,128)(2,1)}), bf16[1024,8192]{0,1:T(8,128)(2,1)}) %all-gather.6.cloned.1.call-update) | async-done | bytes 16777232 | tf_op jit(solution)/shard_map/all_gather | solution.py:85
  410.6 27.9 %reshape.77 = bf16[4,256,8192]{1,0,2:T(4,128)(2,1)} reshape(bf16[1024,8192]{0,1:T(8,128)(2,1)} %all-gather.6.cloned.1.call-done) | data formatting | bytes 33554432 | tf_op jit(solution)/shard_map/all_gather | solution.py:85
  438.4 10.4 %constant_dynamic-slice_fusion = bf16[1,256,8192]{1,0,2:T(2,128)(2,1)S(1)} fusion(bf16[4,256,8192]{1,0,2:T(4,128)(2,1)} %reshape.77, s32[]{:T(128)S(6)} %select_n.60), kind=kLoop, calls=%fused_computation.59 | loop fusion | bytes 8388612 | tf_op jit(solution)/shard_map/jit(dynamic_index_in_dim)/dynamic_slice | solution.py:86
  448.9 10.5 %convert_bitcast_fusion = (bf16[1,1,256,8192]{2,3,1,0:T(8,128)(2,1)}, bf16[1,1,256,8192]{2,3,1,0:T(8,128)(2,1)}) fusion(bf16[1,256,8192]{1,0,2:T(2,128)(2,1)S(1)} %constant_dynamic-slice_fusion, f32[256,8192]{0,1:T(8,128)} %get-tuple-element.23, bf16[1,1,256,8192]{2,3,1,0:T(8,128)(2,1)S(1)} %copy-done, bf16[1,1,256,8192]{2,3,1,0:T(8,128)(2,1)S(1)} %copy-done.1), kind=kLoop, calls=%fused_computation.28 | loop fusion | flops 27262976 | bytes 29360128 | tf_op jit(solution)/shard_map/broadcast_in_dim | solution.py:98
  459.4 6.3 %copy.89 = bf16[1,1,256,8192]{3,2,1,0:T(8,128)(2,1)} copy(bf16[1,1,256,8192]{2,3,1,0:T(8,128)(2,1)} %get-tuple-element.21) | data formatting | bytes 8388608
  465.7 6.3 %copy.90 = bf16[1,1,256,8192]{3,2,1,0:T(8,128)(2,1)} copy(bf16[1,1,256,8192]{2,3,1,0:T(8,128)(2,1)} %get-tuple-element.20) | data formatting | bytes 8388608
  (42 shorter events, 9.1 us)
Async XLA Ops:
  7.2 52.8 %copy-start.4 = (bf16[1,1,128,4,256]{4,3,2,1,0:T(4,128)(2,1)S(1)}, bf16[1,1,128,4,256]{4,3,2,1,0:T(4,128)(2,1)}, u32[]{:S(2)}) copy-start(bf16[1,1,128,4,256]{4,3,2,1,0:T(4,128)(2,1)} %param.7) | copy-start | bytes 786436
  7.2 127.6 %all-gather.4.cloned.1.call-start = ((), (), s32[]{:S(2)}) async-start(), calls=%async_computation.3 | async-start | bytes 8912896 | tf_op jit(solution)/shard_map/all_gather | solution.py:72
  11.9 24.0 %collective-permute-start.1 = (bf16[4,8,2,8192]{3,0,2,1:T(4,128)(2,1)S(1)}, bf16[4,8,2,8192]{3,0,2,1:T(4,128)(2,1)S(1)}, u32[]{:S(2)}, u32[]{:S(2)}) collective-permute-start(bf16[4,8,2,8192]{3,0,2,1:T(4,128)(2,1)S(1)} %fusion.5), channel_id=1, source_target_pairs={{16,0},{17,1},{18,2},{19,3},{20,4},{21,5},{22,6},{23,7},{24,8},{25... | collective-permute-start | bytes 3145736 | tf_op jit(solution)/shard_map/ppermute | solution.py:16
  59.9 179.3 %reduce-scatter.4.cloned.1.call-start = ((), (), s32[]{:S(2)}) async-start(), calls=%async_computation.5 | async-start | bytes 8912896
  75.3 335.2 %all-gather.6.cloned.1.call-start = ((), (), s32[]{:S(2)}) async-start(), calls=%async_computation.4 | async-start | bytes 20971520 | tf_op jit(solution)/shard_map/all_gather | solution.py:85
  81.9 71.6 %copy-start.5 = (s32[4,2]{0,1:T(2,128)S(1)}, s32[4,2]{0,1:T(2,128)}, u32[]{:S(2)}) copy-start(s32[4,2]{0,1:T(2,128)} %param.10) | copy-start | bytes 100
  81.9 157.3 %copy-start.2 = (bf16[1,1,8,4,8192]{4,3,2,1,0:T(4,128)(2,1)S(1)}, bf16[1,1,8,4,8192]{4,3,2,1,0:T(4,128)(2,1)}, u32[]{:S(2)}) copy-start(bf16[1,1,8,4,8192]{4,3,2,1,0:T(4,128)(2,1)} %param.6) | copy-start | bytes 1572868
  153.5 118.6 %copy-start.6 = (s32[4,2]{0,1:T(2,128)S(1)}, s32[4,2]{0,1:T(2,128)}, u32[]{:S(2)}) copy-start(s32[4,2]{0,1:T(2,128)} %param.11) | copy-start | bytes 100
  239.2 59.5 %copy-start.3 = (bf16[8,32768]{1,0:T(8,128)(2,1)S(1)}, bf16[8,32768]{1,0:T(8,128)(2,1)}, u32[]{:S(2)}) copy-start(bf16[8,32768]{1,0:T(8,128)(2,1)} %reduce-scatter.4.cloned.1.call-done) | copy-start | bytes 1572868
  241.9 25.9 %collective-permute-start = (bf16[4,8,2,8192]{3,2,1,0:T(2,128)(2,1)S(1)}, bf16[4,8,2,8192]{3,2,1,0:T(2,128)(2,1)}, u32[]{:S(2)}, u32[]{:S(2)}) collective-permute-start(bf16[4,8,2,8192]{3,2,1,0:T(2,128)(2,1)S(1)} %broadcast_multiply_fusion), channel_id=1, source_target_pairs={{0,16},{1,17},{2,18},{3,19},{4,20},{5,21},{6,22},{7,23},{8,24},{9,... | collective-permute-start | bytes 3145736 | tf_op jit(solution)/shard_map/ppermute | solution.py:16
  267.8 30.9 %all-to-all-start = ((bf16[4,8,2,8192]{3,2,1,0:T(2,128)(2,1)}), bf16[4,8,2,8192]{3,2,1,0:T(2,128)(2,1)S(1)}, u32[]{:S(2)}, u32[]{:S(2)}) async-start(bf16[4,8,2,8192]{3,2,1,0:T(2,128)(2,1)} %collective-permute-done), calls=%async_computation | async-start | bytes 2097152 | tf_op jit(solution)/shard_map/all_to_all | solution.py:67
  438.4 10.4 %copy-start = (bf16[1,1,256,8192]{2,3,1,0:T(8,128)(2,1)S(1)}, bf16[1,1,256,8192]{2,3,1,0:T(8,128)(2,1)}, u32[]{:S(2)}) copy-start(bf16[1,1,256,8192]{2,3,1,0:T(8,128)(2,1)} %copy.73) | copy-start | bytes 12582916
  438.4 10.4 %copy-start.1 = (bf16[1,1,256,8192]{2,3,1,0:T(8,128)(2,1)S(1)}, bf16[1,1,256,8192]{2,3,1,0:T(8,128)(2,1)}, u32[]{:S(2)}) copy-start(bf16[1,1,256,8192]{2,3,1,0:T(8,128)(2,1)} %copy.84) | copy-start | bytes 12582916
Sparse Core Ops, SparseCore 0:
  60.0 74.7 all-gather.3
  139.0 100.1 reduce-scatter.3
  241.4 169.0 all-gather.5
where the time goes:
time: 480 us; the launch traced here: 479 us
  waiting for transfers between devices  296 us (62%)
  local copies, waits for them, and re-layouts  75.5 us (16%)
  matrix products  45.1 us (9%)
  blocking collectives  19.1 us (4%)
  other arithmetic  17.7 us (4%)
  between operations  16.5 us (3%)
  starting transfers between devices  8.21 us (2%)
    all_gather x1, waiting for transfers between devices, local(): gathered = lax.all_gather(message[None], 'replica', axis=0, tiled=True)  94.2 us
    unnamed x4, waiting for transfers between devices  85.5 us
    all_gather x1, waiting for transfers between devices, local(): row_piece = lax.all_gather(cot_here, 'tensor', axis=0, tiled=True)  52.9 us
    ppermute x2, waiting for transfers between devices, passed_along(): return lax.ppermute(array, axis, pairs)  46.3 us
    unnamed x21, local copies, waits for them, and re-layouts  34.7 us
    all_gather x1, local copies, waits for them, and re-layouts, local(): gathered = lax.all_gather(message[None], 'replica', axis=0, tiled=True)  27.9 us
    all_to_all x1, blocking collectives, local(): lax.all_to_all(moved_back, 'replica', split_axis=0, concat_axis=0, tiled=...  19.1 us
    dot_general x1, matrix products, local(): jnp.einsum('tkh,tkd->hd', ctx_rows, row_piece, preferred_element_type=jnp...  18.7 us
  transfers between devices with their start and end apart: 6, of which 6 were waited for; matrix products, arithmetic and copies ran while one was open for 14% of the time, Pallas kernels for 0%

commit v1 on v0

v1 whole, which is shorter than its diff:
```python
import functools
import math

import jax
import jax.numpy as jnp
from jax import lax
from jax.experimental import pallas as pl
from jax.experimental.pallas import tpu as pltpu
from jax.sharding import PartitionSpec as P

ALPHA = 0.9
GAMMA = 0.5
BETA_SCALE = 0.4
CHUNKS = 8
TILE = 512
MESH = pl.DeviceIdType.MESH
BF16 = jnp.bfloat16
F32 = jnp.float32


def loop(n, body):
    def step(i, carry):
        body(i)
        return carry

    lax.fori_loop(0, n, step, 0)


def dot(a, b):
    return jnp.dot(a, b, preferred_element_type=F32)


def kernel(
    beta, width, route, partner, bnd, ctx, w_hbm, m_hbm, so, cg_out, nw_hbm, nm_hbm,
    w, mom, ctx_t, cg, cot, msg, g1, st, g2, part, prec, rrec, bsum, bsend, brecv, fr, sel_b, sel_f, mask,
    ag_s, ag_r, rs_s, rs_r, bk_s, bk_r, fw_s, fw_r, yb_s, yb_r, yf_s, yf_r, cf_s, cf_r, cp_s, cp_r,
    p1_s, p1_r, p2_s, p2_r, w_i, m_i, w_o, m_o,
):
    rep = lax.axis_index("replica")
    sec = lax.axis_index("section")
    ten = lax.axis_index("tensor")
    chip = lax.div(ten, 2)
    core = lax.rem(ten, 2)
    z = lax.div(chip, 2)
    high = lax.rem(chip, 2)
    other = 1 - core
    sibling = (rep, sec, 2 * chip + other)
    right = (lax.rem(rep + 1, 4), sec, ten)
    left = (lax.rem(rep + 3, 4), sec, ten)
    across = (rep, 1 - sec, ten)

    def chip_at(e):
        return lax.rem(z + lax.div(e, 2), 4) * 2 + lax.rem(high + lax.rem(e, 2), 2)

    def rep_at(e):
        return lax.rem(rep + e, 4)

    def peer(e):
        return (rep, sec, 2 * chip_at(e) + core)

    def send(src, dst, ss, rs, to):
        pltpu.make_async_remote_copy(
            src_ref=src, dst_ref=dst, send_sem=ss, recv_sem=rs, device_id=to, device_id_type=MESH
        ).start()

    def sent(ref, sem):
        pltpu.make_async_remote_copy(
            src_ref=ref, dst_ref=ref, send_sem=sem, recv_sem=sem, device_id=sibling, device_id_type=MESH
        ).wait_send()

    def arrived(ref, sem):
        pltpu.make_async_remote_copy(
            src_ref=ref, dst_ref=ref, send_sem=sem, recv_sem=sem, device_id=sibling, device_id_type=MESH
        ).wait_recv()

    def columns(k):
        return pl.ds(pl.multiple_of(k * width, width), width)

    def tiles(body):
        loop(width // TILE, lambda j: body(pl.ds(pl.multiple_of(j * TILE, TILE), TILE)))

    def w_in(k):
        return pltpu.make_async_copy(w_hbm.at[:, columns(k)], w.at[k], w_i.at[k])

    def m_in(k):
        return pltpu.make_async_copy(m_hbm.at[:, columns(k)], mom.at[k], m_i.at[k])

    def w_out(k):
        return pltpu.make_async_copy(w.at[k], nw_hbm.at[:, columns(k)], w_o.at[k])

    def m_out(k):
        return pltpu.make_async_copy(mom.at[k], nm_hbm.at[:, columns(k)], m_o.at[k])

    barrier = pltpu.get_barrier_semaphore()

    def greet(to):
        pl.semaphore_signal(barrier, inc=1, device_id=to, device_id_type=MESH)

    greet(sibling)
    greet(across)
    for e in range(1, 4):
        greet((rep_at(e), sec, ten))
    loop(7, lambda e: greet(peer(e + 1)))
    loop(CHUNKS, lambda k: w_in(k).start())
    loop(CHUNKS, lambda k: m_in(k).start())

    cg[...] = jnp.zeros_like(cg)
    ctx_t[...] = ctx[...].reshape(512, 256).T

    routes = [route[j // 2, j % 2] for j in range(8)]
    slots = []
    for j in range(8):
        before = jnp.int32(0)
        for i in range(j):
            before = before + jnp.where(routes[i] == routes[j], 1, 0)
        slots.append(before)
    count = jnp.int32(0)
    for j in range(8):
        count = count + jnp.where(routes[j] == rep, 1, 0)

    def selector(shape, wide, narrow):
        a = lax.broadcasted_iota(jnp.int32, shape, wide)
        b = lax.broadcasted_iota(jnp.int32, shape, narrow)
        same = jnp.where((a % 16) // 2 == (b % 16) // 2, 1.0, 0.0)
        pair = (a // 16) * 2 + a % 2
        slot = (b // 16) * 2 + b % 2
        total = jnp.zeros(shape, F32)
        for j in range(8):
            mine = jnp.where(routes[j] == rep, 1.0, 0.0).astype(F32)
            total = total + mine * jnp.where((pair == j) & (slot == slots[j]), same, 0.0)
        return total.astype(BF16)

    sel_b[...] = selector((64, 32), 0, 1)
    sel_f[...] = selector((32, 64), 1, 0)
    rows = lax.broadcasted_iota(jnp.int32, (32, 128), 0)
    mask[...] = jnp.where((rows // 16) * 2 + rows % 2 < count, 1.0, 0.0)

    @pl.when(sec == 0)
    def _():
        def clear(k):
            loop(8, lambda c: cot.at[k, core, c, pl.ds(16, 16)].__setitem__(..., jnp.zeros((16, width), BF16)))

        loop(CHUNKS, clear)

    as_one = lambda flag: jnp.where(flag, 1.0, 0.0).astype(F32)
    own_right = as_one(partner[rep_at(1), sec] == rep)
    own_left = as_one(partner[rep_at(3), sec] == rep)
    mine = partner[rep, sec]
    from_left = as_one(mine == rep_at(3))
    from_right = as_one(mine == rep_at(1))
    from_far = as_one(mine == rep_at(2))

    pl.semaphore_wait(barrier, 12)

    def gather(k, count_rows):
        block = cot.at[k, core, chip, pl.ds(0, count_rows)]
        loop(7, lambda e: send(block, block, ag_s.at[k, e], ag_r.at[k, chip], peer(e + 1)))

    def route_back(k):
        cot_rows = bnd[:, columns(k)]
        bsend[k] = dot(sel_b[...], cot_rows).astype(BF16).reshape(4, 16, width)
        for e in (1, 3, 2):
            to = rep_at(e)
            send(bsend.at[k, to], brecv.at[k, rep], bk_s.at[k, e], bk_r.at[k, rep], (to, sec, ten))
        cot[k, core, chip] = (cot_rows.astype(F32) * mask[:, 0:1]).astype(BF16)
        gather(k, 32)

    def cross_back(k):
        total = bsend[k, rep].astype(F32)
        for e in (1, 3, 2):
            source = rep_at(e)
            arrived(brecv.at[k, source], bk_r.at[k, source])
            total = total + brecv[k, source].astype(F32)
        bsend[k, rep] = total.astype(BF16)
        send(bsend.at[k, rep], cot.at[k, core, chip, pl.ds(0, 16)], yb_s.at[k], yb_r.at[k], across)

    def gather_first(k):
        arrived(cot.at[k, core, chip, pl.ds(0, 16)], yb_r.at[k])
        gather(k, 16)

    def share(k):
        def wait_rows(count_rows):
            def one(e):
                source = chip_at(e + 1)
                arrived(cot.at[k, core, source, pl.ds(0, count_rows)], ag_r.at[k, source])

            loop(7, one)

        pl.when(sec == 0)(lambda: wait_rows(16))
        pl.when(sec == 1)(lambda: wait_rows(32))
        send(cot.at[k, core], cot.at[k, core], cf_s.at[k], cf_r.at[k], sibling)

    def cot_tile(k, cols):
        return cot[k, :, :, :, cols].reshape(512, TILE)

    def message(k):
        arrived(cot.at[k, other], cf_r.at[k])
        w_in(k).wait()

        def one(cols):
            grad = dot(ctx_t[...], cot_tile(k, cols))
            out = beta * grad - GAMMA * w[k, :, cols].astype(F32)
            msg[k, :, :, cols] = out.astype(BF16).reshape(2, 128, TILE)

        tiles(one)
        send(msg.at[k, 0], g1.at[k, 0], p1_s.at[k, 0], p1_r.at[k, 0], right)
        send(msg.at[k, 1], g1.at[k, 1], p1_s.at[k, 1], p1_r.at[k, 1], left)

    def context_part(k):
        def one(cols):
            cg[...] += lax.dot_general(
                cot_tile(k, cols), w[k, :, cols], (((1,), (1,)), ((), ())), preferred_element_type=F32
            )

        tiles(one)

    def pass_on(k):
        arrived(g1.at[k, 0], p1_r.at[k, 0])

        def one(cols):
            mixed = own_right * msg[k, 1, :, cols].astype(F32) + (1.0 - own_right) * g1[k, 0, :, cols].astype(F32)
            st[k, 0, :, cols] = mixed.astype(BF16)

        tiles(one)
        send(st.at[k, 0], g2.at[k, 0], p2_s.at[k, 0], p2_r.at[k, 0], right)
        arrived(g1.at[k, 1], p1_r.at[k, 1])

        def two(cols):
            mixed = own_left * msg[k, 0, :, cols].astype(F32) + (1.0 - own_left) * g1[k, 1, :, cols].astype(F32)
            st[k, 1, :, cols] = mixed.astype(BF16)

        tiles(two)
        send(st.at[k, 1], g2.at[k, 1], p2_s.at[k, 1], p2_r.at[k, 1], left)

    def update(k):
        arrived(g2.at[k, 0], p2_r.at[k, 0])
        arrived(g2.at[k, 1], p2_r.at[k, 1])
        m_in(k).wait()

        def one(cols):
            grad = dot(ctx_t[...], cot_tile(k, cols))
            a1, b1 = g1[k, 0, :, cols].astype(F32), g1[k, 1, :, cols].astype(F32)
            a2, b2 = g2[k, 0, :, cols].astype(F32), g2[k, 1, :, cols].astype(F32)
            top = from_left * a1 + from_right * b2 + from_far * a2
            low = from_left * a2 + from_right * b1 + from_far * b2
            for half, theirs in ((0, top), (128, low)):
                at = pl.ds(half, 128)
                current = w[k, at, cols].astype(F32)
                delta = (
                    ALPHA * mom[k, at, cols].astype(F32)
                    - 0.5 * (beta * grad[half : half + 128] + GAMMA * current)
                    - 0.5 * theirs
                )
                mom[k, at, cols] = delta.astype(BF16)
                w[k, at, cols] = (current + delta).astype(BF16)

        tiles(one)
        w_out(k).start()
        m_out(k).start()

    def branch_far(k):
        def one(cols):
            part[k, :, :, cols] = dot(ctx[other], w[k, :, cols]).astype(BF16).reshape(8, 32, TILE)

        tiles(one)
        send(part.at[k], prec.at[k], cp_s.at[k], cp_r.at[k], sibling)

    def branch_near(k):
        arrived(prec.at[k], cp_r.at[k])

        def one(cols):
            own = dot(ctx[core], w[k, :, cols]).reshape(8, 32, TILE)
            prec[k, :, :, cols] = (own + prec[k, :, :, cols].astype(F32)).astype(BF16)

        tiles(one)

        def spread(count_rows):
            def one_peer(e):
                block = prec.at[k, chip_at(e + 1), pl.ds(0, count_rows)]
                to = rrec.at[k, chip, pl.ds(0, count_rows)]
                send(block, to, rs_s.at[k, e], rs_r.at[k, chip], peer(e + 1))

            loop(7, one_peer)

        pl.when(sec == 0)(lambda: spread(16))
        pl.when(sec == 1)(lambda: spread(32))

    def reduce_rows(k, count_rows):
        at = pl.ds(0, count_rows)

        def wait_one(e):
            source = chip_at(e + 1)
            arrived(rrec.at[k, source, at], rs_r.at[k, source])

        loop(7, wait_one)
        total = prec[k, chip, at].astype(F32)
        for e in range(1, 8):
            total = total + rrec[k, chip_at(e), at].astype(F32)
        return total

    def reduce_first(k):
        total = reduce_rows(k, 16)
        stream = (bnd[pl.ds(0, 16), columns(k)].astype(F32) + total).astype(BF16)
        so[pl.ds(0, 16), columns(k)] = stream
        so[pl.ds(16, 16), columns(k)] = jnp.zeros_like(stream)
        fr[k, rep] = stream
        send(fr.at[k, rep], fr.at[k, rep], yf_s.at[k], yf_r.at[k], across)

    def reduce_second(k):
        bsum[k] = reduce_rows(k, 32)

    def route_ahead(k):
        arrived(fr.at[k, rep], yf_r.at[k])
        for e in (1, 3, 2):
            to = rep_at(e)
            send(fr.at[k, rep], fr.at[k, rep], fw_s.at[k, e], fw_r.at[k, rep], (to, sec, ten))

    def finish_second(k):
        for e in (1, 3, 2):
            source = rep_at(e)
            arrived(fr.at[k, source], fw_r.at[k, source])
        total = dot(sel_f[...], fr[k].reshape(64, width)) + bsum[k]
        so[:, columns(k)] = (total.astype(BF16).astype(F32) * mask[:, 0:1]).astype(BF16)

    late = 1 - sec
    stages = (
        (0, 1, route_back),
        (1, 1, cross_back),
        (2, 0, gather_first),
        (2 + late, None, share),
        (3 + late, None, message),
        (4 + late, None, pass_on),
        (3 + late, None, context_part),
        (3 + late, None, branch_far),
        (4 + late, None, branch_near),
        (5 + late, None, update),
        (5 + late, 0, reduce_first),
        (5 + late, 1, reduce_second),
        (6, 1, route_ahead),
        (7, 1, finish_second),
    )

    def step(i):
        for lag, only, stage in stages:
            k = i - lag
            live = (k >= 0) & (k < CHUNKS)
            if only is not None:
                live = live & (sec == only)
            pl.when(live)(functools.partial(stage, k))

    loop(CHUNKS + 7, step)

    cg_out[...] = cg[...].astype(BF16)

    def drain(k):
        def rows_sent(count_rows):
            def one(e):
                sent(cot.at[k, core, chip, pl.ds(0, count_rows)], ag_s.at[k, e])
                sent(prec.at[k, chip, pl.ds(0, count_rows)], rs_s.at[k, e])

            loop(7, one)

        @pl.when(sec == 0)
        def _():
            rows_sent(16)
            sent(fr.at[k, rep], yf_s.at[k])

        @pl.when(sec == 1)
        def _():
            rows_sent(32)
            sent(bsend.at[k, rep], yb_s.at[k])
            for e in (1, 2, 3):
                sent(bsend.at[k, rep], bk_s.at[k, e])
                sent(fr.at[k, rep], fw_s.at[k, e])

        sent(cot.at[k, core], cf_s.at[k])
        sent(part.at[k], cp_s.at[k])
        for half in (0, 1):
            sent(msg.at[k, half], p1_s.at[k, half])
            sent(st.at[k, half], p2_s.at[k, half])
        w_out(k).wait()
        m_out(k).wait()

    loop(CHUNKS, drain)


def local(boundary, context, weights, momentum, route, partner):
    beta = BETA_SCALE / math.sqrt(512)
    model = weights.shape[-1]
    width = model // CHUNKS
    bnd = boundary.reshape(8, 2, 2, model).transpose(1, 0, 2, 3).reshape(32, model)
    ctx = context.reshape(8, 2, 8, 2, 2, 256).transpose(1, 0, 3, 2, 4, 5).reshape(2, 256, 256)
    n = CHUNKS
    dma = pltpu.SemaphoreType.DMA
    scratch = [
        pltpu.VMEM((n, 256, width), BF16),
        pltpu.VMEM((n, 256, width), BF16),
        pltpu.VMEM((256, 512), BF16),
        pltpu.VMEM((512, 256), F32),
        pltpu.VMEM((n, 2, 8, 32, width), BF16),
        pltpu.VMEM((n, 2, 128, width), BF16),
        pltpu.VMEM((n, 2, 128, width), BF16),
        pltpu.VMEM((n, 2, 128, width), BF16),
        pltpu.VMEM((n, 2, 128, width), BF16),
        pltpu.VMEM((n, 8, 32, width), BF16),
        pltpu.VMEM((n, 8, 32, width), BF16),
        pltpu.VMEM((n, 8, 32, width), BF16),
        pltpu.VMEM((n, 32, width), F32),
        pltpu.VMEM((n, 4, 16, width), BF16),
        pltpu.VMEM((n, 4, 16, width), BF16),
        pltpu.VMEM((n, 4, 16, width), BF16),
        pltpu.VMEM((64, 32), BF16),
        pltpu.VMEM((32, 64), BF16),
        pltpu.VMEM((32, 128), F32),
        *[dma((n, 8))] * 4,
        *[dma((n, 4))] * 4,
        *[dma((n,))] * 8,
        *[dma((n, 2))] * 4,
        *[dma((n,))] * 4,
    ]
    vmem = pl.BlockSpec(memory_space=pltpu.VMEM)
    smem = pl.BlockSpec(memory_space=pltpu.SMEM)
    anywhere = pl.BlockSpec(memory_space=pl.ANY)
    stream, ctx_grad, new_weights, new_momentum = pl.pallas_call(
        functools.partial(kernel, beta, width),
        out_shape=(
            jax.ShapeDtypeStruct((32, model), BF16),
            jax.ShapeDtypeStruct((512, 256), BF16),
            jax.ShapeDtypeStruct((256, model), BF16),
            jax.ShapeDtypeStruct((256, model), BF16),
        ),
        in_specs=[smem, smem, vmem, vmem, anywhere, anywhere],
        out_specs=(vmem, vmem, anywhere, anywhere),
        scratch_shapes=scratch,
        compiler_params=pltpu.CompilerParams(
            collective_id=0, has_side_effects=True, vmem_limit_bytes=62 * 2**20
        ),
        name="noloco_step",
    )(route, partner, bnd, ctx, weights[0, 0], momentum[0, 0])
    stream = stream.reshape(2, 8, 2, model).transpose(1, 0, 2, 3).reshape(1, 1, 8, 4, model)
    ctx_grad = ctx_grad.reshape(2, 8, 2, 8, 2, 256).transpose(1, 0, 3, 2, 4, 5).reshape(1, 1, 128, 4, 256)
    return stream, ctx_grad, new_weights[None, None], new_momentum[None, None]


def solution(mesh):
    in_specs = (
        P("replica", "section", "tensor", None, None),
        P("replica", "section", None, None, "tensor"),
        P("replica", "section", "tensor", None),
        P("replica", "section", "tensor", None),
        P(),
        P(),
    )
    out_specs = (
        P("replica", "section", "tensor", None, None),
        P("replica", "section", None, None, "tensor"),
        P("replica", "section", "tensor", None),
        P("replica", "section", "tensor", None),
    )
    return jax.shard_map(local, mesh=mesh, in_specs=in_specs, out_specs=out_specs, check_vma=False)
```

time: 480 us -> 164 us (0.34)
  waiting for transfers between devices: 296 us -> 0 us
  Pallas kernels: 0 us -> 144 us
  local copies, waits for them, and re-layouts: 75.5 us -> 19.6 us
  matrix products: 45.1 us -> 0 us
  blocking collectives: 19.1 us -> 0 us
  other arithmetic: 17.7 us -> 0 us
  between operations: 16.5 us -> 0.7 us
  starting transfers between devices: 8.21 us -> 0 us
    all_gather x2 -> x0, waiting for transfers between devices: 147 us -> none  [the longest x1 94.2 us: local(): gathered = lax.all_gather(message[None], 'replica', axis=0, tiled=True)]
    pallas_call x0 -> x1, Pallas kernels: none -> 144 us  [local(): pl.pallas_call(functools.partial(kernel, beta, width), out_shape=(jax.Sha...]
    unnamed x4 -> x0, waiting for transfers between devices: 85.5 us -> none
    ppermute x2 -> x0, waiting for transfers between devices: 46.3 us -> none  [passed_along(): return lax.ppermute(array, axis, pairs)]
    dot_general x5 -> x0, matrix products: 45.1 us -> none  [the longest x1 18.7 us: local(): jnp.einsum('tkh,tkd->hd', ctx_rows, row_piece, preferred_element_type=jnp...]
    all_gather x1 -> x0, local copies, waits for them, and re-layouts: 27.9 us -> none  [local(): gathered = lax.all_gather(message[None], 'replica', axis=0, tiled=True)]
    unnamed x21 -> x6, local copies, waits for them, and re-layouts: 34.7 us -> 9.48 us
    all_to_all x1 -> x0, blocking collectives: 19.1 us -> none  [local(): lax.all_to_all(moved_back, 'replica', split_axis=0, concat_axis=0, tiled=...]
  transfers between devices with their start and end apart: 6 -> 0, of which waited for: 6 -> 0; matrix products, arithmetic and copies ran while one was open for 14% -> 0% of each run, Pallas kernels for 0% -> 0%
where the time goes in v1:
time: 164 us
  Pallas kernels  144 us (88%)
  local copies, waits for them, and re-layouts  19.6 us (12%)
    pallas_call x1, Pallas kernels, local(): pl.pallas_call(functools.partial(kernel, beta, width), out_shape=(jax.Sha...  144 us
    unnamed x6, local copies, waits for them, and re-layouts  9.48 us

profile of v1, /device:TPU:8, one launch (start us, length us, event | category | flops | bytes accessed | tf_op | source)
XLA Modules:
  0.0 164.0 jit_solution(6202671185144754734)
XLA Ops:
  0.6 1.3 copy.12.route
  2.0 1.3 copy.13.partner
  3.3 1.1 reshape.34
  4.4 0.2 copy.19
  4.6 0.8 reshape.35.ctx
  5.4 1.8 %reshape.32 = bf16[8,2,2,8192]{3,2,1,0:T(2,128)(2,1)S(1)} reshape(bf16[1,1,8,4,8192]{4,3,2,1,0:T(4,128)(2,1)} %param.6) | data formatting | bytes 1048576 | tf_op jit(solution)/shard_map/reshape | solution.py:391
  7.2 0.4 copy.18
  7.6 1.0 reshape.33.bnd
  8.6 143.7 %noloco_step.1 = (bf16[32,8192]{1,0:T(8,128)(2,1)}, bf16[512,256]{1,0:T(8,128)(2,1)}, bf16[256,8192]{1,0:T(8,128)(2,1)}, bf16[256,8192]{1,0:T(8,128)(2,1)}) custom-call(s32[4,2]{1,0:T(4,128)} %copy.12.route, s32[4,2]{1,0:T(4,128)} %copy.13.partner, bf16[32,8192]{1,0:T(8,128)(2,1)} %reshape.33.bnd, bf16[2,256,256]{2,1,0:T(8,128)(2,1)} %reshape.35.ctx, ...), custom_call_target="tpu_custom_call" | custom-call | tf_op jit(solution)/shard_map/noloco_step/pallas_call | solution.py:424
  152.3 1.4 reshape.36
  153.7 0.4 copy.14
  154.1 1.0 reshape.37
  155.1 1.1 reshape.38
  156.1 0.2 copy.15
  156.3 0.8 reshape.39
  157.2 0.0 copy-start
  157.2 4.8 %copy.22 = bf16[1,1,256,8192]{3,2,1,0:T(8,128)(2,1)} copy(bf16[1,1,256,8192]{3,2,1,0:T(8,128)(2,1)} %bitcast.15) | data formatting | bytes 8388608
  162.0 0.0 copy-done
  162.0 2.0 %copy.23 = bf16[1,1,256,8192]{3,2,1,0:T(8,128)(2,1)} copy(bf16[1,1,256,8192]{3,2,1,0:T(8,128)(2,1)S(1)} %bitcast.14) | data formatting | bytes 8388608
Async XLA Ops:
  157.2 4.8 %copy-start = (bf16[256,8192]{1,0:T(8,128)(2,1)S(1)}, bf16[256,8192]{1,0:T(8,128)(2,1)}, u32[]{:S(2)}) copy-start(bf16[256,8192]{1,0:T(8,128)(2,1)} %get-tuple-element.11) | copy-start | bytes 12582916

commit v2 on v1

--- a/solution.py
+++ b/solution.py
@@ -12,6 +12,7 @@
 GAMMA = 0.5
 BETA_SCALE = 0.4
 CHUNKS = 8
+AHEAD = 8
 TILE = 512
 MESH = pl.DeviceIdType.MESH
 BF16 = jnp.bfloat16
@@ -31,10 +32,10 @@
 
 
 def kernel(
-    beta, width, route, partner, bnd, ctx, w_hbm, m_hbm, so, cg_out, nw_hbm, nm_hbm,
-    w, mom, ctx_t, cg, cot, msg, g1, st, g2, part, prec, rrec, bsum, bsend, brecv, fr, sel_b, sel_f, mask,
+    beta, width, route, partner, bnd, ctx, w_hbm, m_hbm, so, cg_out, w, mom,
+    ctx_t, cg, cot, msg, g1, st, g2, part, prec, rrec, bsum, bsend, brecv, fr, yb, sel_b, sel_f, mask,
     ag_s, ag_r, rs_s, rs_r, bk_s, bk_r, fw_s, fw_r, yb_s, yb_r, yf_s, yf_r, cf_s, cf_r, cp_s, cp_r,
-    p1_s, p1_r, p2_s, p2_r, w_i, m_i, w_o, m_o,
+    p1_s, p1_r, p2_s, p2_r, w_i, m_i,
 ):
     rep = lax.axis_index("replica")
     sec = lax.axis_index("section")
@@ -79,17 +80,18 @@
     def tiles(body):
         loop(width // TILE, lambda j: body(pl.ds(pl.multiple_of(j * TILE, TILE), TILE)))
 
+    def model(k, body):
+        def one(j):
+            whole = pl.multiple_of(k * width + j * TILE, TILE)
+            body(pl.ds(pl.multiple_of(j * TILE, TILE), TILE), pl.ds(whole, TILE))
+
+        loop(width // TILE, one)
+
     def w_in(k):
-        return pltpu.make_async_copy(w_hbm.at[:, columns(k)], w.at[k], w_i.at[k])
+        return pltpu.make_async_copy(w_hbm.at[:, columns(k)], w.at[:, columns(k)], w_i.at[k])
 
     def m_in(k):
-        return pltpu.make_async_copy(m_hbm.at[:, columns(k)], mom.at[k], m_i.at[k])
-
-    def w_out(k):
-        return pltpu.make_async_copy(w.at[k], nw_hbm.at[:, columns(k)], w_o.at[k])
-
-    def m_out(k):
-        return pltpu.make_async_copy(mom.at[k], nm_hbm.at[:, columns(k)], m_o.at[k])
+        return pltpu.make_async_copy(m_hbm.at[:, columns(k)], mom.at[:, columns(k)], m_i.at[k])
 
     barrier = pltpu.get_barrier_semaphore()
 
@@ -104,10 +106,7 @@
     loop(CHUNKS, lambda k: w_in(k).start())
     loop(CHUNKS, lambda k: m_in(k).start())
 
-    cg[...] = jnp.zeros_like(cg)
-    ctx_t[...] = ctx[...].reshape(512, 256).T
-
-    routes = [route[j // 2, j % 2] for j in range(8)]
+    routes = [route[j % 2, j // 2] for j in range(8)]
     slots = []
     for j in range(8):
         before = jnp.int32(0)
@@ -121,9 +120,8 @@
     def selector(shape, wide, narrow):
         a = lax.broadcasted_iota(jnp.int32, shape, wide)
         b = lax.broadcasted_iota(jnp.int32, shape, narrow)
-        same = jnp.where((a % 16) // 2 == (b % 16) // 2, 1.0, 0.0)
-        pair = (a // 16) * 2 + a % 2
-        slot = (b // 16) * 2 + b % 2
+        same = jnp.where(a % 8 == b % 8, 1.0, 0.0)
+        pair, slot = a // 8, b // 8
         total = jnp.zeros(shape, F32)
         for j in range(8):
             mine = jnp.where(routes[j] == rep, 1.0, 0.0).astype(F32)
@@ -131,21 +129,13 @@
         return total.astype(BF16)
 
     sel_b[...] = selector((64, 32), 0, 1)
-    sel_f[...] = selector((32, 64), 1, 0)
     rows = lax.broadcasted_iota(jnp.int32, (32, 128), 0)
-    mask[...] = jnp.where((rows // 16) * 2 + rows % 2 < count, 1.0, 0.0)
-
-    @pl.when(sec == 0)
-    def _():
-        def clear(k):
-            loop(8, lambda c: cot.at[k, core, c, pl.ds(16, 16)].__setitem__(..., jnp.zeros((16, width), BF16)))
-
-        loop(CHUNKS, clear)
+    mask[...] = jnp.where(rows // 8 < count, 1.0, 0.0)
 
     as_one = lambda flag: jnp.where(flag, 1.0, 0.0).astype(F32)
-    own_right = as_one(partner[rep_at(1), sec] == rep)
-    own_left = as_one(partner[rep_at(3), sec] == rep)
-    mine = partner[rep, sec]
+    own_right = as_one(partner[sec, rep_at(1)] == rep)
+    own_left = as_one(partner[sec, rep_at(3)] == rep)
+    mine = partner[sec, rep]
     from_left = as_one(mine == rep_at(3))
     from_right = as_one(mine == rep_at(1))
     from_far = as_one(mine == rep_at(2))
@@ -157,13 +147,10 @@
         loop(7, lambda e: send(block, block, ag_s.at[k, e], ag_r.at[k, chip], peer(e + 1)))
 
     def route_back(k):
-        cot_rows = bnd[:, columns(k)]
-        bsend[k] = dot(sel_b[...], cot_rows).astype(BF16).reshape(4, 16, width)
+        bsend[k] = dot(sel_b[...], bnd[:, columns(k)]).astype(BF16).reshape(4, 16, width)
         for e in (1, 3, 2):
             to = rep_at(e)
             send(bsend.at[k, to], brecv.at[k, rep], bk_s.at[k, e], bk_r.at[k, rep], (to, sec, ten))
-        cot[k, core, chip] = (cot_rows.astype(F32) * mask[:, 0:1]).astype(BF16)
-        gather(k, 32)
 
     def cross_back(k):
         total = bsend[k, rep].astype(F32)
@@ -171,12 +158,16 @@
             source = rep_at(e)
             arrived(brecv.at[k, source], bk_r.at[k, source])
             total = total + brecv[k, source].astype(F32)
-        bsend[k, rep] = total.astype(BF16)
-        send(bsend.at[k, rep], cot.at[k, core, chip, pl.ds(0, 16)], yb_s.at[k], yb_r.at[k], across)
+        yb[k] = total.astype(BF16)
+        send(yb.at[k], cot.at[k, core, chip, pl.ds(0, 16)], yb_s.at[k], yb_r.at[k], across)
 
     def gather_first(k):
         arrived(cot.at[k, core, chip, pl.ds(0, 16)], yb_r.at[k])
         gather(k, 16)
+
+    def gather_second(k):
+        cot[k, core, chip] = (bnd[:, columns(k)].astype(F32) * mask[:, 0:1]).astype(BF16)
+        gather(k, 32)
 
     def share(k):
         def wait_rows(count_rows):
@@ -195,24 +186,23 @@
 
     def message(k):
         arrived(cot.at[k, other], cf_r.at[k])
-        w_in(k).wait()
-
-        def one(cols):
+
+        def one(cols, whole):
             grad = dot(ctx_t[...], cot_tile(k, cols))
-            out = beta * grad - GAMMA * w[k, :, cols].astype(F32)
+            out = beta * grad - GAMMA * w[:, whole].astype(F32)
             msg[k, :, :, cols] = out.astype(BF16).reshape(2, 128, TILE)
 
-        tiles(one)
+        model(k, one)
         send(msg.at[k, 0], g1.at[k, 0], p1_s.at[k, 0], p1_r.at[k, 0], right)
         send(msg.at[k, 1], g1.at[k, 1], p1_s.at[k, 1], p1_r.at[k, 1], left)
 
     def context_part(k):
-        def one(cols):
+        def one(cols, whole):
             cg[...] += lax.dot_general(
-                cot_tile(k, cols), w[k, :, cols], (((1,), (1,)), ((), ())), preferred_element_type=F32
+                cot_tile(k, cols), w[:, whole], (((1,), (1,)), ((), ())), preferred_element_type=F32
             )
 
-        tiles(one)
+        model(k, one)
 
     def pass_on(k):
         arrived(g1.at[k, 0], p1_r.at[k, 0])
@@ -237,7 +227,7 @@
         arrived(g2.at[k, 1], p2_r.at[k, 1])
         m_in(k).wait()
 
-        def one(cols):
+        def one(cols, whole):
             grad = dot(ctx_t[...], cot_tile(k, cols))
             a1, b1 = g1[k, 0, :, cols].astype(F32), g1[k, 1, :, cols].astype(F32)
             a2, b2 = g2[k, 0, :, cols].astype(F32), g2[k, 1, :, cols].astype(F32)
@@ -245,34 +235,32 @@
             low = from_left * a2 + from_right * b1 + from_far * b2
             for half, theirs in ((0, top), (128, low)):
                 at = pl.ds(half, 128)
-                current = w[k, at, cols].astype(F32)
+                current = w[at, whole].astype(F32)
                 delta = (
-                    ALPHA * mom[k, at, cols].astype(F32)
+                    ALPHA * mom[at, whole].astype(F32)
                     - 0.5 * (beta * grad[half : half + 128] + GAMMA * current)
                     - 0.5 * theirs
                 )
-                mom[k, at, cols] = delta.astype(BF16)
-                w[k, at, cols] = (current + delta).astype(BF16)
-
-        tiles(one)
-        w_out(k).start()
-        m_out(k).start()
+                mom[at, whole] = delta.astype(BF16)
+                w[at, whole] = (current + delta).astype(BF16)
+
+        model(k, one)
 
     def branch_far(k):
-        def one(cols):
-            part[k, :, :, cols] = dot(ctx[other], w[k, :, cols]).astype(BF16).reshape(8, 32, TILE)
-
-        tiles(one)
+        def one(cols, whole):
+            part[k, :, :, cols] = dot(ctx[other], w[:, whole]).astype(BF16).reshape(8, 32, TILE)
+
+        model(k, one)
         send(part.at[k], prec.at[k], cp_s.at[k], cp_r.at[k], sibling)
 
     def branch_near(k):
         arrived(prec.at[k], cp_r.at[k])
 
-        def one(cols):
-            own = dot(ctx[core], w[k, :, cols]).reshape(8, 32, TILE)
+        def one(cols, whole):
+            own = dot(ctx[core], w[:, whole]).reshape(8, 32, TILE)
             prec[k, :, :, cols] = (own + prec[k, :, :, cols].astype(F32)).astype(BF16)
 
-        tiles(one)
+        model(k, one)
 
         def spread(count_rows):
             def one_peer(e):
@@ -322,33 +310,58 @@
         total = dot(sel_f[...], fr[k].reshape(64, width)) + bsum[k]
         so[:, columns(k)] = (total.astype(BF16).astype(F32) * mask[:, 0:1]).astype(BF16)
 
+    @pl.when(sec == 1)
+    def _():
+        route_back(0)
+        gather_second(0)
+        loop(CHUNKS - 1, lambda k: route_back(k + 1))
+
+    cg[...] = jnp.zeros_like(cg)
+    ctx_t[...] = ctx[...].reshape(512, 256).T
+    sel_f[...] = selector((32, 64), 1, 0)
+
+    @pl.when(sec == 0)
+    def _():
+        def clear(k):
+            loop(8, lambda c: cot.at[k, core, c, pl.ds(16, 16)].__setitem__(..., jnp.zeros((16, width), BF16)))
+
+        loop(CHUNKS, clear)
+
     late = 1 - sec
     stages = (
-        (0, 1, route_back),
-        (1, 1, cross_back),
-        (2, 0, gather_first),
-        (2 + late, None, share),
-        (3 + late, None, message),
+        (2, None, lambda k: w_in(k).wait()),
+        (2 + late, None, message),
         (4 + late, None, pass_on),
-        (3 + late, None, context_part),
-        (3 + late, None, branch_far),
-        (4 + late, None, branch_near),
-        (5 + late, None, update),
-        (5 + late, 0, reduce_first),
-        (5 + late, 1, reduce_second),
-        (6, 1, route_ahead),
-        (7, 1, finish_second),
+        (1, 0, gather_first),
+        (None, 1, cross_back),
+        (-1, 1, gather_second),
+        (1 + late, None, share),
+        (2, None, branch_far),
+        (4, None, branch_near),
+        (6, 0, reduce_first),
+        (6, 1, reduce_second),
+        (AHEAD, 1, route_ahead),
+        (AHEAD + 2, 1, finish_second),
+        (2 + late, None, context_part),
+        (6 + late, None, update),
     )
+
+    def run(live, only, stage, k):
+        live = live & (k < CHUNKS)
+        if only is not None:
+            live = live & (sec == only)
+        pl.when(live)(functools.partial(stage, k))
 
     def step(i):
         for lag, only, stage in stages:
-            k = i - lag
-            live = (k >= 0) & (k < CHUNKS)
-            if only is not None:
-                live = live & (sec == only)
-            pl.when(live)(functools.partial(stage, k))
-
-    loop(CHUNKS + 7, step)
+            if lag is None:
+                run(i >= 1, only, stage, 2 * i - 1)
+                run(i >= 0, only, stage, 2 * i)
+            else:
+                k = i - lag
+                run((k >= 0) & (i >= 0), only, stage, k)
+
+    loop(CHUNKS + AHEAD + 2, step)
 
     cg_out[...] = cg[...].astype(BF16)
 
@@ -368,7 +381,7 @@
         @pl.when(sec == 1)
         def _():
             rows_sent(32)
-            sent(bsend.at[k, rep], yb_s.at[k])
+            sent(yb.at[k], yb_s.at[k])
             for e in (1, 2, 3):
                 sent(bsend.at[k, rep], bk_s.at[k, e])
                 sent(fr.at[k, rep], fw_s.at[k, e])
@@ -378,8 +391,6 @@
         for half in (0, 1):
             sent(msg.at[k, half], p1_s.at[k, half])
             sent(st.at[k, half], p2_s.at[k, half])
-        w_out(k).wait()
-        m_out(k).wait()
 
     loop(CHUNKS, drain)
 
@@ -388,13 +399,11 @@
     beta = BETA_SCALE / math.sqrt(512)
     model = weights.shape[-1]
     width = model // CHUNKS
-    bnd = boundary.reshape(8, 2, 2, model).transpose(1, 0, 2, 3).reshape(32, model)
-    ctx = context.reshape(8, 2, 8, 2, 2, 256).transpose(1, 0, 3, 2, 4, 5).reshape(2, 256, 256)
+    bnd = boundary.reshape(8, 4, model).transpose(1, 0, 2).reshape(32, model)
+    ctx = context.reshape(8, 2, 8, 4, 256).transpose(1, 0, 3, 2, 4).reshape(2, 256, 256)
     n = CHUNKS
     dma = pltpu.SemaphoreType.DMA
     scratch = [
-        pltpu.VMEM((n, 256, width), BF16),
-        pltpu.VMEM((n, 256, width), BF16),
         pltpu.VMEM((256, 512), BF16),
         pltpu.VMEM((512, 256), F32),
         pltpu.VMEM((n, 2, 8, 32, width), BF16),
@@ -409,6 +418,7 @@
         pltpu.VMEM((n, 4, 16, width), BF16),
         pltpu.VMEM((n, 4, 16, width), BF16),
         pltpu.VMEM((n, 4, 16, width), BF16),
+        pltpu.VMEM((n, 16, width), BF16),
         pltpu.VMEM((64, 32), BF16),
         pltpu.VMEM((32, 64), BF16),
         pltpu.VMEM((32, 128), F32),
@@ -416,7 +426,7 @@
         *[dma((n, 4))] * 4,
         *[dma((n,))] * 8,
         *[dma((n, 2))] * 4,
-        *[dma((n,))] * 4,
+        *[dma((n,))] * 2,
     ]
     vmem = pl.BlockSpec(memory_space=pltpu.VMEM)
     smem = pl.BlockSpec(memory_space=pltpu.SMEM)
@@ -424,21 +434,21 @@
     stream, ctx_grad, new_weights, new_momentum = pl.pallas_call(
         functools.partial(kernel, beta, width),
         out_shape=(
-            jax.ShapeDtypeStruct((32, model), BF16),
-            jax.ShapeDtypeStruct((512, 256), BF16),
-            jax.ShapeDtypeStruct((256, model), BF16),
-            jax.ShapeDtypeStruct((256, model), BF16),
+            pltpu.VMEM((32, model), BF16),
+            pltpu.VMEM((512, 256), BF16),
+            pltpu.VMEM((256, model), BF16),
+            pltpu.VMEM((256, model), BF16),
         ),
         in_specs=[smem, smem, vmem, vmem, anywhere, anywhere],
-        out_specs=(vmem, vmem, anywhere, anywhere),
+        out_specs=(vmem, vmem, vmem, vmem),
         scratch_shapes=scratch,
         compiler_params=pltpu.CompilerParams(
-            collective_id=0, has_side_effects=True, vmem_limit_bytes=62 * 2**20
+            collective_id=0, has_side_effects=True, vmem_limit_bytes=48 * 2**20
         ),
         name="noloco_step",
-    )(route, partner, bnd, ctx, weights[0, 0], momentum[0, 0])
-    stream = stream.reshape(2, 8, 2, model).transpose(1, 0, 2, 3).reshape(1, 1, 8, 4, model)
-    ctx_grad = ctx_grad.reshape(2, 8, 2, 8, 2, 256).transpose(1, 0, 3, 2, 4, 5).reshape(1, 1, 128, 4, 256)
+    )(route.T, partner.T, bnd, ctx, weights[0, 0], momentum[0, 0])
+    stream = stream.reshape(4, 8, model).transpose(1, 0, 2).reshape(1, 1, 8, 4, model)
+    ctx_grad = ctx_grad.reshape(2, 8, 4, 8, 256).transpose(1, 0, 3, 2, 4).reshape(1, 1, 128, 4, 256)
     return stream, ctx_grad, new_weights[None, None], new_momentum[None, None]
 
 

time: 164 us -> 143 us (0.87)
  Pallas kernels: 144 us -> 132 us
  local copies, waits for them, and re-layouts: 19.6 us -> 9.87 us
    pallas_call x1, Pallas kernels: 144 us -> 132 us  [local(): pl.pallas_call(functools.partial(kernel, beta, width), out_shape=(pltpu.V...]
    reshape x10 -> x2, local copies, waits for them, and re-layouts: 9.52 us -> 2.89 us  [the longest x1 1.69 us: local(): context.reshape(8, 2, 8, 4, 256).transpose(1, 0, 3, 2, 4)]
    unnamed x6 -> x2, local copies, waits for them, and re-layouts: 9.48 us -> 4.03 us
    transpose x2, local copies, waits for them, and re-layouts: 0.59 us -> 2.95 us  [the longest x1 2.13 us: local(): bnd = boundary.reshape(8, 4, model).transpose(1, 0, 2).reshape(32, model)]
where the time goes in v2:
time: 143 us; the launch traced here: 142 us
  Pallas kernels  132 us (92%)
  local copies, waits for them, and re-layouts  9.87 us (7%)
    pallas_call x1, Pallas kernels, local(): pl.pallas_call(functools.partial(kernel, beta, width), out_shape=(pltpu.V...  132 us
    unnamed x2, local copies, waits for them, and re-layouts  4.03 us

profile of v2, /device:TPU:8, one launch (start us, length us, event | category | flops | bytes accessed | tf_op | source)
XLA Modules:
  0.0 142.3 jit_solution(13185247988190854237)
XLA Ops:
  0.6 1.7 %copy.11 = bf16[8,2,8,4,256]{4,2,3,0,1:T(8,128)(2,1)} copy(bf16[8,2,8,4,256]{4,3,2,1,0:T(4,128)(2,1)} %bitcast.36) | data formatting | bytes 524288 | tf_op jit(solution)/shard_map/reshape | solution.py:403
  2.3 2.1 %copy.17 = bf16[4,8,8192]{2,1,0:T(8,128)(2,1)} copy(bf16[4,8,8192]{2,0,1:T(4,128)(2,1)} %bitcast.34) | data formatting | bytes 1048576 | tf_op jit(solution)/shard_map/transpose | solution.py:402
  4.4 131.8 %noloco_step.1 = (bf16[32,8192]{1,0:T(8,128)(2,1)S(1)}, bf16[512,256]{1,0:T(8,128)(2,1)S(1)}, bf16[256,8192]{1,0:T(8,128)(2,1)S(1)}, bf16[256,8192]{1,0:T(8,128)(2,1)S(1)}) custom-call(s32[2,4]{1,0:T(2,128)} %bitcast.38, s32[2,4]{1,0:T(2,128)} %bitcast.39, bf16[32,8192]{1,0:T(8,128)(2,1)} %bitcast.32, bf16[2,256,256]{2,1,0:T(8,128)(2,1)} %bitcast.33, ...), custom_call_target="tpu_custom_call" | custom-call | tf_op jit(solution)/shard_map/noloco_step/pallas_call | solution.py:434
  136.3 1.2 copy.16
  137.5 0.8 copy.13
  138.3 2.0 %copy.20 = bf16[1,1,256,8192]{3,2,1,0:T(8,128)(2,1)} copy(bf16[1,1,256,8192]{3,2,1,0:T(8,128)(2,1)S(1)} %bitcast.27) | data formatting | bytes 8388608
  140.3 2.0 %copy.21 = bf16[1,1,256,8192]{3,2,1,0:T(8,128)(2,1)} copy(bf16[1,1,256,8192]{3,2,1,0:T(8,128)(2,1)S(1)} %bitcast.26) | data formatting | bytes 8388608

commit v3 on v2

--- a/solution.py
+++ b/solution.py
@@ -11,7 +11,7 @@
 ALPHA = 0.9
 GAMMA = 0.5
 BETA_SCALE = 0.4
-CHUNKS = 8
+CHUNKS = 16
 AHEAD = 8
 TILE = 512
 MESH = pl.DeviceIdType.MESH
@@ -74,6 +74,9 @@
             src_ref=ref, dst_ref=ref, send_sem=sem, recv_sem=sem, device_id=sibling, device_id_type=MESH
         ).wait_recv()
 
+    def seven(ref, count_rows):
+        return ref.at[pl.ds(0, 7), pl.ds(0, count_rows)]
+
     def columns(k):
         return pl.ds(pl.multiple_of(k * width, width), width)
 
@@ -144,22 +147,21 @@
 
     def gather(k, count_rows):
         block = cot.at[k, core, chip, pl.ds(0, count_rows)]
-        loop(7, lambda e: send(block, block, ag_s.at[k, e], ag_r.at[k, chip], peer(e + 1)))
+        loop(7, lambda e: send(block, block, ag_s.at[k], ag_r.at[k], peer(e + 1)))
 
     def route_back(k):
         bsend[k] = dot(sel_b[...], bnd[:, columns(k)]).astype(BF16).reshape(4, 16, width)
         for e in (1, 3, 2):
             to = rep_at(e)
-            send(bsend.at[k, to], brecv.at[k, rep], bk_s.at[k, e], bk_r.at[k, rep], (to, sec, ten))
+            send(bsend.at[k, to], brecv.at[k, rep], bk_s.at[k], bk_r.at[k], (to, sec, ten))
 
     def cross_back(k):
         total = bsend[k, rep].astype(F32)
+        arrived(brecv.at[k, pl.ds(0, 3)], bk_r.at[k])
         for e in (1, 3, 2):
-            source = rep_at(e)
-            arrived(brecv.at[k, source], bk_r.at[k, source])
-            total = total + brecv[k, source].astype(F32)
-        yb[k] = total.astype(BF16)
-        send(yb.at[k], cot.at[k, core, chip, pl.ds(0, 16)], yb_s.at[k], yb_r.at[k], across)
+            total = total + brecv[k, rep_at(e)].astype(F32)
+        yb[k, 0] = total.astype(BF16)
+        send(yb.at[k, 0], cot.at[k, core, chip, pl.ds(0, 16)], yb_s.at[k], yb_r.at[k], across)
 
     def gather_first(k):
         arrived(cot.at[k, core, chip, pl.ds(0, 16)], yb_r.at[k])
@@ -170,15 +172,8 @@
         gather(k, 32)
 
     def share(k):
-        def wait_rows(count_rows):
-            def one(e):
-                source = chip_at(e + 1)
-                arrived(cot.at[k, core, source, pl.ds(0, count_rows)], ag_r.at[k, source])
-
-            loop(7, one)
-
-        pl.when(sec == 0)(lambda: wait_rows(16))
-        pl.when(sec == 1)(lambda: wait_rows(32))
+        pl.when(sec == 0)(lambda: arrived(seven(cot.at[k, core], 16), ag_r.at[k]))
+        pl.when(sec == 1)(lambda: arrived(seven(cot.at[k, core], 32), ag_r.at[k]))
         send(cot.at[k, core], cot.at[k, core], cf_s.at[k], cf_r.at[k], sibling)
 
     def cot_tile(k, cols):
@@ -193,8 +188,8 @@
             msg[k, :, :, cols] = out.astype(BF16).reshape(2, 128, TILE)
 
         model(k, one)
-        send(msg.at[k, 0], g1.at[k, 0], p1_s.at[k, 0], p1_r.at[k, 0], right)
-        send(msg.at[k, 1], g1.at[k, 1], p1_s.at[k, 1], p1_r.at[k, 1], left)
+        send(msg.at[k, 0], g1.at[k, 0], p1_s.at[k], p1_r.at[k, 0], right)
+        send(msg.at[k, 1], g1.at[k, 1], p1_s.at[k], p1_r.at[k, 1], left)
 
     def context_part(k):
         def one(cols, whole):
@@ -212,7 +207,7 @@
             st[k, 0, :, cols] = mixed.astype(BF16)
 
         tiles(one)
-        send(st.at[k, 0], g2.at[k, 0], p2_s.at[k, 0], p2_r.at[k, 0], right)
+        send(st.at[k, 0], g2.at[k, 0], p2_s.at[k], p2_r.at[k], right)
         arrived(g1.at[k, 1], p1_r.at[k, 1])
 
         def two(cols):
@@ -220,11 +215,10 @@
             st[k, 1, :, cols] = mixed.astype(BF16)
 
         tiles(two)
-        send(st.at[k, 1], g2.at[k, 1], p2_s.at[k, 1], p2_r.at[k, 1], left)
+        send(st.at[k, 1], g2.at[k, 1], p2_s.at[k], p2_r.at[k], left)
 
     def update(k):
-        arrived(g2.at[k, 0], p2_r.at[k, 0])
-        arrived(g2.at[k, 1], p2_r.at[k, 1])
+        arrived(g2.at[k], p2_r.at[k])
         m_in(k).wait()
 
         def one(cols, whole):
@@ -266,7 +260,7 @@
             def one_peer(e):
                 block = prec.at[k, chip_at(e + 1), pl.ds(0, count_rows)]
                 to = rrec.at[k, chip, pl.ds(0, count_rows)]
-                send(block, to, rs_s.at[k, e], rs_r.at[k, chip], peer(e + 1))
+                send(block, to, rs_s.at[k], rs_r.at[k], peer(e + 1))
 
             loop(7, one_peer)
 
@@ -276,15 +270,22 @@
     def reduce_rows(k, count_rows):
         at = pl.ds(0, count_rows)
 
-        def wait_one(e):
-            source = chip_at(e + 1)
-            arrived(rrec.at[k, source, at], rs_r.at[k, source])
-
-        loop(7, wait_one)
+        arrived(seven(rrec.at[k], count_rows), rs_r.at[k])
         total = prec[k, chip, at].astype(F32)
         for e in range(1, 8):
             total = total + rrec[k, chip_at(e), at].astype(F32)
         return total
+
+    def sorted_first(k):
+        return (k >= 2) & (k < 8)
+
+    def spread_first(k):
+        for e in (1, 3, 2):
+            to = rep_at(e)
+            send(fr.at[k, rep], fr.at[k, rep], fw_s.at[k], fw_r.at[k], (to, sec, ten))
+
+    def all_first(k):
+        arrived(fr.at[k, pl.ds(0, 3)], fw_r.at[k])
 
     def reduce_first(k):
         total = reduce_rows(k, 16)
@@ -292,23 +293,45 @@
         so[pl.ds(0, 16), columns(k)] = stream
         so[pl.ds(16, 16), columns(k)] = jnp.zeros_like(stream)
         fr[k, rep] = stream
-        send(fr.at[k, rep], fr.at[k, rep], yf_s.at[k], yf_r.at[k], across)
+
+        @pl.when(sorted_first(k))
+        def _():
+            spread_first(k)
+
+        @pl.when(jnp.logical_not(sorted_first(k)))
+        def _():
+            send(fr.at[k, rep], fr.at[k, rep], yf_s.at[k], yf_r.at[k], across)
 
     def reduce_second(k):
         bsum[k] = reduce_rows(k, 32)
 
     def route_ahead(k):
-        arrived(fr.at[k, rep], yf_r.at[k])
-        for e in (1, 3, 2):
-            to = rep_at(e)
-            send(fr.at[k, rep], fr.at[k, rep], fw_s.at[k, e], fw_r.at[k, rep], (to, sec, ten))
+        @pl.when(jnp.logical_not(sorted_first(k)))
+        def _():
+            arrived(fr.at[k, rep], yf_r.at[k])
+            spread_first(k)
+
+    def sort_first(k):
+        @pl.when(sorted_first(k))
+        def _():
+            all_first(k)
+            yb[k] = dot(sel_f[...], fr[k].reshape(64, width)).astype(BF16).reshape(2, 16, width)
+            send(yb.at[k], fr.at[k, pl.ds(0, 2)], yf_s.at[k], yf_r.at[k], across)
+
+    def put_second(k, arriving):
+        total = arriving + bsum[k]
+        so[:, columns(k)] = (total.astype(BF16).astype(F32) * mask[:, 0:1]).astype(BF16)
 
     def finish_second(k):
-        for e in (1, 3, 2):
-            source = rep_at(e)
-            arrived(fr.at[k, source], fw_r.at[k, source])
-        total = dot(sel_f[...], fr[k].reshape(64, width)) + bsum[k]
-        so[:, columns(k)] = (total.astype(BF16).astype(F32) * mask[:, 0:1]).astype(BF16)
+        @pl.when(sorted_first(k))
+        def _():
+            arrived(fr.at[k, pl.ds(0, 2)], yf_r.at[k])
+            put_second(k, fr[k, pl.ds(0, 2)].reshape(32, width).astype(F32))
+
+        @pl.when(jnp.logical_not(sorted_first(k)))
+        def _():
+            all_first(k)
+            put_second(k, dot(sel_f[...], fr[k].reshape(64, width)))
 
     @pl.when(sec == 1)
     def _():
@@ -326,6 +349,42 @@
             loop(8, lambda c: cot.at[k, core, c, pl.ds(16, 16)].__setitem__(..., jnp.zeros((16, width), BF16)))
 
         loop(CHUNKS, clear)
+
+    def first_sent(k):
+        sent(fr.at[k, pl.ds(0, 3)], fw_s.at[k])
+
+    def drain(k):
+        def rows_sent(count_rows):
+            sent(seven(cot.at[k, core], count_rows), ag_s.at[k])
+            sent(seven(prec.at[k], count_rows), rs_s.at[k])
+
+        @pl.when(sec == 0)
+        def _():
+            rows_sent(16)
+
+            @pl.when(sorted_first(k))
+            def _():
+                sent(yb.at[k], yf_s.at[k])
+                first_sent(k)
+
+            @pl.when(jnp.logical_not(sorted_first(k)))
+            def _():
+                sent(fr.at[k, rep], yf_s.at[k])
+
+        @pl.when(sec == 1)
+        def _():
+            rows_sent(32)
+            sent(yb.at[k, 0], yb_s.at[k])
+            sent(bsend.at[k, pl.ds(0, 3)], bk_s.at[k])
+
+            @pl.when(jnp.logical_not(sorted_first(k)))
+            def _():
+                first_sent(k)
+
+        sent(cot.at[k, core], cf_s.at[k])
+        sent(part.at[k], cp_s.at[k])
+        sent(msg.at[k], p1_s.at[k])
+        sent(st.at[k], p2_s.at[k])
 
     late = 1 - sec
     stages = (
@@ -341,9 +400,11 @@
         (6, 0, reduce_first),
         (6, 1, reduce_second),
         (AHEAD, 1, route_ahead),
+        (AHEAD, 0, sort_first),
         (AHEAD + 2, 1, finish_second),
         (2 + late, None, context_part),
         (6 + late, None, update),
+        (AHEAD + 2, None, drain),
     )
 
     def run(live, only, stage, k):
@@ -364,35 +425,6 @@
     loop(CHUNKS + AHEAD + 2, step)
 
     cg_out[...] = cg[...].astype(BF16)
-
-    def drain(k):
-        def rows_sent(count_rows):
-            def one(e):
-                sent(cot.at[k, core, chip, pl.ds(0, count_rows)], ag_s.at[k, e])
-                sent(prec.at[k, chip, pl.ds(0, count_rows)], rs_s.at[k, e])
-
-            loop(7, one)
-
-        @pl.when(sec == 0)
-        def _():
-            rows_sent(16)
-            sent(fr.at[k, rep], yf_s.at[k])
-
-        @pl.when(sec == 1)
-        def _():
-            rows_sent(32)
-            sent(yb.at[k], yb_s.at[k])
-            for e in (1, 2, 3):
-                sent(bsend.at[k, rep], bk_s.at[k, e])
-                sent(fr.at[k, rep], fw_s.at[k, e])
-
-        sent(cot.at[k, core], cf_s.at[k])
-        sent(part.at[k], cp_s.at[k])
-        for half in (0, 1):
-            sent(msg.at[k, half], p1_s.at[k, half])
-            sent(st.at[k, half], p2_s.at[k, half])
-
-    loop(CHUNKS, drain)
 
 
 def local(boundary, context, weights, momentum, route, partner):
@@ -418,15 +450,13 @@
         pltpu.VMEM((n, 4, 16, width), BF16),
         pltpu.VMEM((n, 4, 16, width), BF16),
         pltpu.VMEM((n, 4, 16, width), BF16),
-        pltpu.VMEM((n, 16, width), BF16),
+        pltpu.VMEM((n, 2, 16, width), BF16),
         pltpu.VMEM((64, 32), BF16),
         pltpu.VMEM((32, 64), BF16),
         pltpu.VMEM((32, 128), F32),
-        *[dma((n, 8))] * 4,
-        *[dma((n, 4))] * 4,
-        *[dma((n,))] * 8,
-        *[dma((n, 2))] * 4,
-        *[dma((n,))] * 2,
+        *[dma((n,))] * 17,
+        dma((n, 2)),
+        *[dma((n,))] * 4,
     ]
     vmem = pl.BlockSpec(memory_space=pltpu.VMEM)
     smem = pl.BlockSpec(memory_space=pltpu.SMEM)

time: 143 us -> 135 us (0.944)
  Pallas kernels: 132 us -> 124 us
    pallas_call x1, Pallas kernels: 132 us -> 124 us  [local(): pl.pallas_call(functools.partial(kernel, beta, width), out_shape=(pltpu.V...]
where the time goes in v3:
time: 135 us
  Pallas kernels  124 us (92%)
  local copies, waits for them, and re-layouts  9.87 us (7%)
    pallas_call x1, Pallas kernels, local(): pl.pallas_call(functools.partial(kernel, beta, width), out_shape=(pltpu.V...  124 us
    unnamed x2, local copies, waits for them, and re-layouts  4.03 us

profile of v3, /device:TPU:8, one launch (start us, length us, event | category | flops | bytes accessed | tf_op | source)
XLA Modules:
  0.0 134.9 jit_solution(12424166030032088663)
XLA Ops:
  0.6 1.7 %copy.11 = bf16[8,2,8,4,256]{4,2,3,0,1:T(8,128)(2,1)} copy(bf16[8,2,8,4,256]{4,3,2,1,0:T(4,128)(2,1)} %bitcast.36) | data formatting | bytes 524288 | tf_op jit(solution)/shard_map/reshape | solution.py:435
  2.3 2.1 %copy.17 = bf16[4,8,8192]{2,1,0:T(8,128)(2,1)} copy(bf16[4,8,8192]{2,0,1:T(4,128)(2,1)} %bitcast.34) | data formatting | bytes 1048576 | tf_op jit(solution)/shard_map/transpose | solution.py:434
  4.4 124.4 %noloco_step.1 = (bf16[32,8192]{1,0:T(8,128)(2,1)S(1)}, bf16[512,256]{1,0:T(8,128)(2,1)S(1)}, bf16[256,8192]{1,0:T(8,128)(2,1)S(1)}, bf16[256,8192]{1,0:T(8,128)(2,1)S(1)}) custom-call(s32[2,4]{1,0:T(2,128)} %bitcast.38, s32[2,4]{1,0:T(2,128)} %bitcast.39, bf16[32,8192]{1,0:T(8,128)(2,1)} %bitcast.32, bf16[2,256,256]{2,1,0:T(8,128)(2,1)} %bitcast.33, ...), custom_call_target="tpu_custom_call" | custom-call | tf_op jit(solution)/shard_map/noloco_step/pallas_call | solution.py:464
  128.8 1.2 copy.16
  130.0 0.8 copy.13
  130.8 2.0 %copy.20 = bf16[1,1,256,8192]{3,2,1,0:T(8,128)(2,1)} copy(bf16[1,1,256,8192]{3,2,1,0:T(8,128)(2,1)S(1)} %bitcast.27) | data formatting | bytes 8388608
  132.8 2.0 %copy.21 = bf16[1,1,256,8192]{3,2,1,0:T(8,128)(2,1)} copy(bf16[1,1,256,8192]{3,2,1,0:T(8,128)(2,1)S(1)} %bitcast.26) | data formatting | bytes 8388608

commit v4 on v3

--- a/solution.py
+++ b/solution.py
@@ -27,15 +27,23 @@
     lax.fori_loop(0, n, step, 0)
 
 
+def by_slot(block):
+    return jnp.swapaxes(block.astype(F32), 0, 1).reshape(-1, block.shape[-1])
+
+
+def by_token(rows):
+    return jnp.swapaxes(rows.reshape(4, 8, rows.shape[-1]), 0, 1).astype(BF16)
+
+
 def dot(a, b):
     return jnp.dot(a, b, preferred_element_type=F32)
 
 
 def kernel(
-    beta, width, route, partner, bnd, ctx, w_hbm, m_hbm, so, cg_out, w, mom,
-    ctx_t, cg, cot, msg, g1, st, g2, part, prec, rrec, bsum, bsend, brecv, fr, yb, sel_b, sel_f, mask,
+    beta, width, route, partner, own, ctx_hbm, w_hbm, m_hbm, so, cg_out, w, mom,
+    bnd, ctx_in_order, ctx, ctx_t, cg, cot, msg, g1, st, g2, part, prec, rrec, bsum, bsend, brecv, fr, yb, sel_b, sel_f, mask,
     ag_s, ag_r, rs_s, rs_r, bk_s, bk_r, fw_s, fw_r, yb_s, yb_r, yf_s, yf_r, cf_s, cf_r, cp_s, cp_r,
-    p1_s, p1_r, p2_s, p2_r, w_i, m_i,
+    p1_s, p1_r, p2_s, p2_r, w_i, m_i, c_i,
 ):
     rep = lax.axis_index("replica")
     sec = lax.axis_index("section")
@@ -90,11 +98,9 @@
 
         loop(width // TILE, one)
 
-    def w_in(k):
-        return pltpu.make_async_copy(w_hbm.at[:, columns(k)], w.at[:, columns(k)], w_i.at[k])
-
-    def m_in(k):
-        return pltpu.make_async_copy(m_hbm.at[:, columns(k)], mom.at[:, columns(k)], m_i.at[k])
+    w_in = pltpu.make_async_copy(w_hbm, w, w_i)
+    m_in = pltpu.make_async_copy(m_hbm, mom, m_i)
+    ctx_in = pltpu.make_async_copy(ctx_hbm, ctx_in_order, c_i)
 
     barrier = pltpu.get_barrier_semaphore()
 
@@ -106,8 +112,8 @@
     for e in range(1, 4):
         greet((rep_at(e), sec, ten))
     loop(7, lambda e: greet(peer(e + 1)))
-    loop(CHUNKS, lambda k: w_in(k).start())
-    loop(CHUNKS, lambda k: m_in(k).start())
+    ctx_in.start()
+    w_in.start()
 
     routes = [route[j % 2, j // 2] for j in range(8)]
     slots = []
@@ -150,6 +156,7 @@
         loop(7, lambda e: send(block, block, ag_s.at[k], ag_r.at[k], peer(e + 1)))
 
     def route_back(k):
+        bnd[:, columns(k)] = by_slot(own[:, :, columns(k)]).astype(BF16)
         bsend[k] = dot(sel_b[...], bnd[:, columns(k)]).astype(BF16).reshape(4, 16, width)
         for e in (1, 3, 2):
             to = rep_at(e)
@@ -219,7 +226,6 @@
 
     def update(k):
         arrived(g2.at[k], p2_r.at[k])
-        m_in(k).wait()
 
         def one(cols, whole):
             grad = dot(ctx_t[...], cot_tile(k, cols))
@@ -240,6 +246,10 @@
 
         model(k, one)
 
+    def first_update(k):
+        pl.when(k == 0)(lambda: m_in.wait())
+        update(k)
+
     def branch_far(k):
         def one(cols, whole):
             part[k, :, :, cols] = dot(ctx[other], w[:, whole]).astype(BF16).reshape(8, 32, TILE)
@@ -289,9 +299,9 @@
 
     def reduce_first(k):
         total = reduce_rows(k, 16)
-        stream = (bnd[pl.ds(0, 16), columns(k)].astype(F32) + total).astype(BF16)
-        so[pl.ds(0, 16), columns(k)] = stream
-        so[pl.ds(16, 16), columns(k)] = jnp.zeros_like(stream)
+        stream = (by_slot(own[:, :, columns(k)])[0:16] + total).astype(BF16)
+        wide = stream.astype(F32)
+        so[:, :, columns(k)] = by_token(jnp.concatenate([wide, jnp.zeros_like(wide)], axis=0))
         fr[k, rep] = stream
 
         @pl.when(sorted_first(k))
@@ -320,7 +330,7 @@
 
     def put_second(k, arriving):
         total = arriving + bsum[k]
-        so[:, columns(k)] = (total.astype(BF16).astype(F32) * mask[:, 0:1]).astype(BF16)
+        so[:, :, columns(k)] = by_token(total.astype(BF16).astype(F32) * mask[:, 0:1])
 
     def finish_second(k):
         @pl.when(sorted_first(k))
@@ -339,7 +349,15 @@
         gather_second(0)
         loop(CHUNKS - 1, lambda k: route_back(k + 1))
 
+    m_in.start()
     cg[...] = jnp.zeros_like(cg)
+    ctx_in.wait()
+
+    def order_rows(t):
+        block = by_slot(ctx_in_order[pl.ds(t * 8, 8)]).astype(BF16)
+        ctx[lax.rem(t, 2), pl.ds(pl.multiple_of(lax.div(t, 2) * 32, 32), 32)] = block
+
+    loop(16, order_rows)
     ctx_t[...] = ctx[...].reshape(512, 256).T
     sel_f[...] = selector((32, 64), 1, 0)
 
@@ -386,9 +404,9 @@
         sent(msg.at[k], p1_s.at[k])
         sent(st.at[k], p2_s.at[k])
 
+    w_in.wait()
     late = 1 - sec
     stages = (
-        (2, None, lambda k: w_in(k).wait()),
         (2 + late, None, message),
         (4 + late, None, pass_on),
         (1, 0, gather_first),
@@ -403,9 +421,13 @@
         (AHEAD, 0, sort_first),
         (AHEAD + 2, 1, finish_second),
         (2 + late, None, context_part),
-        (6 + late, None, update),
+        (6 + late, None, first_update),
         (AHEAD + 2, None, drain),
     )
+
+    def put_context(t):
+        row = (lax.rem(t, 2) * 8 + lax.div(t, 2)) * 32
+        cg_out[pl.ds(t * 8, 8)] = by_token(cg[pl.ds(pl.multiple_of(row, 32), 32)])
 
     def run(live, only, stage, k):
         live = live & (k < CHUNKS)
@@ -414,6 +436,8 @@
         pl.when(live)(functools.partial(stage, k))
 
     def step(i):
+        pl.when(i == CHUNKS + 4)(lambda: loop(16, put_context))
+
         for lag, only, stage in stages:
             if lag is None:
                 run(i >= 1, only, stage, 2 * i - 1)
@@ -424,18 +448,17 @@
 
     loop(CHUNKS + AHEAD + 2, step)
 
-    cg_out[...] = cg[...].astype(BF16)
-
 
 def local(boundary, context, weights, momentum, route, partner):
     beta = BETA_SCALE / math.sqrt(512)
     model = weights.shape[-1]
     width = model // CHUNKS
-    bnd = boundary.reshape(8, 4, model).transpose(1, 0, 2).reshape(32, model)
-    ctx = context.reshape(8, 2, 8, 4, 256).transpose(1, 0, 3, 2, 4).reshape(2, 256, 256)
     n = CHUNKS
     dma = pltpu.SemaphoreType.DMA
     scratch = [
+        pltpu.VMEM((32, model), BF16),
+        pltpu.VMEM((128, 4, 256), BF16),
+        pltpu.VMEM((2, 256, 256), BF16),
         pltpu.VMEM((256, 512), BF16),
         pltpu.VMEM((512, 256), F32),
         pltpu.VMEM((n, 2, 8, 32, width), BF16),
@@ -456,7 +479,8 @@
         pltpu.VMEM((32, 128), F32),
         *[dma((n,))] * 17,
         dma((n, 2)),
-        *[dma((n,))] * 4,
+        *[dma((n,))] * 2,
+        *[dma] * 3,
     ]
     vmem = pl.BlockSpec(memory_space=pltpu.VMEM)
     smem = pl.BlockSpec(memory_space=pltpu.SMEM)
@@ -464,22 +488,20 @@
     stream, ctx_grad, new_weights, new_momentum = pl.pallas_call(
         functools.partial(kernel, beta, width),
         out_shape=(
-            pltpu.VMEM((32, model), BF16),
-            pltpu.VMEM((512, 256), BF16),
+            pltpu.VMEM((8, 4, model), BF16),
+            pltpu.VMEM((128, 4, 256), BF16),
             pltpu.VMEM((256, model), BF16),
             pltpu.VMEM((256, model), BF16),
         ),
-        in_specs=[smem, smem, vmem, vmem, anywhere, anywhere],
+        in_specs=[smem, smem, vmem, anywhere, anywhere, anywhere],
         out_specs=(vmem, vmem, vmem, vmem),
         scratch_shapes=scratch,
         compiler_params=pltpu.CompilerParams(
-            collective_id=0, has_side_effects=True, vmem_limit_bytes=48 * 2**20
+            collective_id=0, has_side_effects=True, vmem_limit_bytes=50 * 2**20
         ),
         name="noloco_step",
-    )(route.T, partner.T, bnd, ctx, weights[0, 0], momentum[0, 0])
-    stream = stream.reshape(4, 8, model).transpose(1, 0, 2).reshape(1, 1, 8, 4, model)
-    ctx_grad = ctx_grad.reshape(2, 8, 4, 8, 256).transpose(1, 0, 3, 2, 4).reshape(1, 1, 128, 4, 256)
-    return stream, ctx_grad, new_weights[None, None], new_momentum[None, None]
+    )(route.T, partner.T, boundary[0, 0], context[0, 0], weights[0, 0], momentum[0, 0])
+    return stream[None, None], ctx_grad[None, None], new_weights[None, None], new_momentum[None, None]
 
 
 def solution(mesh):

time: 135 us -> 130 us (0.963)
  local copies, waits for them, and re-layouts: 9.87 us -> 5.52 us
    transpose x2 -> x0, local copies, waits for them, and re-layouts: 2.95 us -> none  [the longest x1 2.13 us: local(): bnd = boundary.reshape(8, 4, model).transpose(1, 0, 2).reshape(32, model)]
    reshape x2 -> x0, local copies, waits for them, and re-layouts: 2.89 us -> none  [the longest x1 1.69 us: local(): context.reshape(8, 2, 8, 4, 256).transpose(1, 0, 3, 2, 4)]
    unnamed x2 -> x4, local copies, waits for them, and re-layouts: 4.03 us -> 5.52 us
where the time goes in v4:
time: 130 us
  Pallas kernels  124 us (95%)
  local copies, waits for them, and re-layouts  5.52 us (4%)
    pallas_call x1, Pallas kernels, local(): pl.pallas_call(functools.partial(kernel, beta, width), out_shape=(pltpu.V...  124 us
    unnamed x4, local copies, waits for them, and re-layouts  5.52 us

profile of v4, /device:TPU:8, one launch (start us, length us, event | category | flops | bytes accessed | tf_op | source)
XLA Modules:
  0.0 130.3 jit_solution(11344894688783514723)
XLA Ops:
  0.6 124.1 %noloco_step.1 = (bf16[8,4,8192]{2,1,0:T(4,128)(2,1)S(1)}, bf16[128,4,256]{2,1,0:T(4,128)(2,1)S(1)}, bf16[256,8192]{1,0:T(8,128)(2,1)S(1)}, bf16[256,8192]{1,0:T(8,128)(2,1)S(1)}) custom-call(s32[2,4]{1,0:T(2,128)} %bitcast.18, s32[2,4]{1,0:T(2,128)} %bitcast.19, bf16[8,4,8192]{2,1,0:T(4,128)(2,1)} %bitcast.16, bf16[128,4,256]{2,1,0:T(4,128)(2,1)} %bitcast.17, ...), custom_call_target="tpu_custom_call" | custom-call | tf_op jit(solution)/shard_map/noloco_step/pallas_call | solution.py:488
  124.8 0.8 copy.14
  125.6 0.7 copy.15
  126.3 2.0 %copy.16 = bf16[1,1,256,8192]{3,2,1,0:T(8,128)(2,1)} copy(bf16[1,1,256,8192]{3,2,1,0:T(8,128)(2,1)S(1)} %bitcast.11) | data formatting | bytes 8388608
  128.3 2.0 %copy.17 = bf16[1,1,256,8192]{3,2,1,0:T(8,128)(2,1)} copy(bf16[1,1,256,8192]{3,2,1,0:T(8,128)(2,1)S(1)} %bitcast.10) | data formatting | bytes 8388608

commit v5 on v4

--- a/solution.py
+++ b/solution.py
@@ -40,10 +40,10 @@
 
 
 def kernel(
-    beta, width, route, partner, own, ctx_hbm, w_hbm, m_hbm, so, cg_out, w, mom,
-    bnd, ctx_in_order, ctx, ctx_t, cg, cot, msg, g1, st, g2, part, prec, rrec, bsum, bsend, brecv, fr, yb, sel_b, sel_f, mask,
+    beta, width, route, partner, own_hbm, ctx_hbm, w_hbm, m_hbm, so, cg_out, w, mom,
+    own, bnd, ctx_in_order, ctx, ctx_t, cg, cot, msg, g1, st, g2, part, prec, rrec, bsum, bsend, brecv, fr, yb, sel_b, sel_f, mask,
     ag_s, ag_r, rs_s, rs_r, bk_s, bk_r, fw_s, fw_r, yb_s, yb_r, yf_s, yf_r, cf_s, cf_r, cp_s, cp_r,
-    p1_s, p1_r, p2_s, p2_r, w_i, m_i, c_i,
+    p1_s, p1_r, p2_s, p2_r, w_i, m_i, c_i, b_i,
 ):
     rep = lax.axis_index("replica")
     sec = lax.axis_index("section")
@@ -102,6 +102,8 @@
     m_in = pltpu.make_async_copy(m_hbm, mom, m_i)
     ctx_in = pltpu.make_async_copy(ctx_hbm, ctx_in_order, c_i)
 
+    own_in = pltpu.make_async_copy(own_hbm, own, b_i)
+    own_in.start()
     barrier = pltpu.get_barrier_semaphore()
 
     def greet(to):
@@ -149,11 +151,12 @@
     from_right = as_one(mine == rep_at(1))
     from_far = as_one(mine == rep_at(2))
 
+    own_in.wait()
     pl.semaphore_wait(barrier, 12)
 
     def gather(k, count_rows):
         block = cot.at[k, core, chip, pl.ds(0, count_rows)]
-        loop(7, lambda e: send(block, block, ag_s.at[k], ag_r.at[k], peer(e + 1)))
+        loop(7, lambda e: send(block, block, ag_s.at[k], ag_r.at[k], peer(7 - e)))
 
     def route_back(k):
         bnd[:, columns(k)] = by_slot(own[:, :, columns(k)]).astype(BF16)
@@ -189,14 +192,15 @@
     def message(k):
         arrived(cot.at[k, other], cf_r.at[k])
 
-        def one(cols, whole):
-            grad = dot(ctx_t[...], cot_tile(k, cols))
-            out = beta * grad - GAMMA * w[:, whole].astype(F32)
-            msg[k, :, :, cols] = out.astype(BF16).reshape(2, 128, TILE)
-
-        model(k, one)
-        send(msg.at[k, 0], g1.at[k, 0], p1_s.at[k], p1_r.at[k, 0], right)
-        send(msg.at[k, 1], g1.at[k, 1], p1_s.at[k], p1_r.at[k, 1], left)
+        def one(half, cols, whole):
+            at = pl.ds(half * 128, 128)
+            grad = dot(ctx_t[at, :], cot_tile(k, cols))
+            out = beta * grad - GAMMA * w[at, whole].astype(F32)
+            msg[k, half, :, cols] = out.astype(BF16)
+
+        for half, to in ((0, right), (1, left)):
+            model(k, functools.partial(one, half))
+            send(msg.at[k, half], g1.at[k, half], p1_s.at[k], p1_r.at[k, half], to)
 
     def context_part(k):
         def one(cols, whole):
@@ -456,6 +460,7 @@
     n = CHUNKS
     dma = pltpu.SemaphoreType.DMA
     scratch = [
+        pltpu.VMEM((8, 4, model), BF16),
         pltpu.VMEM((32, model), BF16),
         pltpu.VMEM((128, 4, 256), BF16),
         pltpu.VMEM((2, 256, 256), BF16),
@@ -480,7 +485,7 @@
         *[dma((n,))] * 17,
         dma((n, 2)),
         *[dma((n,))] * 2,
-        *[dma] * 3,
+        *[dma] * 4,
     ]
     vmem = pl.BlockSpec(memory_space=pltpu.VMEM)
     smem = pl.BlockSpec(memory_space=pltpu.SMEM)
@@ -493,7 +498,7 @@
             pltpu.VMEM((256, model), BF16),
             pltpu.VMEM((256, model), BF16),
         ),
-        in_specs=[smem, smem, vmem, anywhere, anywhere, anywhere],
+        in_specs=[smem, smem, anywhere, anywhere, anywhere, anywhere],
         out_specs=(vmem, vmem, vmem, vmem),
         scratch_shapes=scratch,
         compiler_params=pltpu.CompilerParams(

time: 130 us -> 130 us (level)
  no operation moved by 1% of the time
where the time goes in v5:
time: 130 us
  Pallas kernels  124 us (95%)
  local copies, waits for them, and re-layouts  5.52 us (4%)
    pallas_call x1, Pallas kernels, local(): pl.pallas_call(functools.partial(kernel, beta, width), out_shape=(pltpu.V...  124 us
    unnamed x4, local copies, waits for them, and re-layouts  5.52 us

profile of v5, /device:TPU:8, one launch (start us, length us, event | category | flops | bytes accessed | tf_op | source)
XLA Modules:
  0.0 130.0 jit_solution(1556479979412079831)
XLA Ops:
  0.6 123.9 %noloco_step.1 = (bf16[8,4,8192]{2,1,0:T(4,128)(2,1)S(1)}, bf16[128,4,256]{2,1,0:T(4,128)(2,1)S(1)}, bf16[256,8192]{1,0:T(8,128)(2,1)S(1)}, bf16[256,8192]{1,0:T(8,128)(2,1)S(1)}) custom-call(s32[2,4]{1,0:T(2,128)} %bitcast.18, s32[2,4]{1,0:T(2,128)} %bitcast.19, bf16[8,4,8192]{2,1,0:T(4,128)(2,1)} %bitcast.16, bf16[128,4,256]{2,1,0:T(4,128)(2,1)} %bitcast.17, ...), custom_call_target="tpu_custom_call" | custom-call | tf_op jit(solution)/shard_map/noloco_step/pallas_call | solution.py:493
  124.5 0.8 copy.14
  125.3 0.7 copy.15
  126.0 2.0 %copy.16 = bf16[1,1,256,8192]{3,2,1,0:T(8,128)(2,1)} copy(bf16[1,1,256,8192]{3,2,1,0:T(8,128)(2,1)S(1)} %bitcast.11) | data formatting | bytes 8388608
  128.0 2.0 %copy.17 = bf16[1,1,256,8192]{3,2,1,0:T(8,128)(2,1)} copy(bf16[1,1,256,8192]{3,2,1,0:T(8,128)(2,1)S(1)} %bitcast.10) | data formatting | bytes 8388608
